TPU v7x, 128 devices: a whole 4x4x4 slice. The times are simulated.
128 devices in a mesh: leaf: 128 (over y, x, z, core).
Axes of the slice: x: 4, y: 4, z: 4, core: 2. Of those that a mesh axis runs over, the one named last changes fastest.
Arguments:
- charges: bfloat16 [32768, 128, 128], P('leaf'), may hold values from -6 to 6
- basis_in: bfloat16 [32768, 64, 128], P('leaf'), may hold values from -0.5 to 0.5
- basis_out: bfloat16 [32768, 64, 128], P('leaf'), may hold values from -0.75 to 0.75
- transfer: bfloat16 [4096, 8, 64, 64], P('leaf'), may hold values from -0.375 to 0.375
- leaf_coupling: bfloat16 [16, 64, 64], replicated, may hold values from -0.25 to 0.25
- parent_coupling: bfloat16 [16, 64, 64], replicated, may hold values from -0.25 to 0.25
- leaf_sources: int32 [32768, 16], P('leaf'), may hold values from 0 to 511, as said below
- leaf_counts: int32 [32768], P('leaf'), may hold values from 2 to 16
- leaf_sends: int32 [128, 2, 128], replicated, may hold values from 0 to 255, as said below
- parent_sources: int32 [4096, 16], P('leaf'), may hold values from 0 to 159, as said below
- parent_counts: int32 [4096], P('leaf'), may hold values from 12 to 16
- parent_sends: int32 [128, 128], replicated, may hold values from 0 to 31
Outputs:
- potential: bfloat16 [32768, 128, 128], P('leaf')
Inputs may be any that keep to these rules, and one draw needn't show every extreme that they name: `leaf_sources`: every row of a device's leaf pool is read by some used slot of that device's leaf lists. `leaf_sends`: the 128 leaves offered in one direction are distinct. `parent_sources`: every row of a device's parent pool is read by some used slot of that device's parent lists.
All inputs are finite; a program needn't handle non-finite values.
Results may differ from a plain program's by a relative error of at most 0.007.
Values may be sent and summed in bfloat16 or wider, within the bound.
No kernel may reach another device: no remote copies, remote signals or barrier semaphores. Data moves between devices by JAX's collectives and lax.ppermute only.
A program may use at most 256 MiB of HBM per device.

v0:
```python
import math

import jax
import jax.numpy as jnp
from jax import lax
from jax.sharding import PartitionSpec as P


def extended_2(value, sides, width):
    for axis, dim in sides:
        size, length = (lax.axis_size(axis), value.shape[dim])
        up = [(i, (i + 1) % size) for i in range(size - 1)]
        down = [(j, i) for i, j in up]
        last = lax.slice_in_dim(value, length - width, length, axis=dim)
        first = lax.slice_in_dim(value, 0, width, axis=dim)
        before = lax.ppermute(last, axis, up)
        after = lax.ppermute(first, axis, down)
        value = jnp.concatenate([before, value, after], axis=dim)
    return value


def pooled_product(pool_rows, sources, counts, coupling):
    target_rows, list_width = sources.shape
    rank_width = coupling.shape[1]
    rhs_width = pool_rows.shape[-1]
    pool_size = pool_rows.shape[0]
    extended = jnp.concatenate(
        [pool_rows, jnp.zeros((1, rank_width, rhs_width), pool_rows.dtype)], 0
    )
    stacked = jnp.transpose(coupling, (1, 0, 2)).reshape(rank_width, list_width * rank_width)
    block_rows = math.gcd(target_rows, 32)
    blocks = target_rows // block_rows

    def one_block(pieces):
        picked_rows, limits = pieces
        valid_mask = lax.broadcasted_iota(jnp.int32, picked_rows.shape, 1) < limits[:, None]
        redirected = jnp.where(valid_mask, picked_rows, pool_size)
        gathered = extended[redirected]
        flattened = gathered.reshape(block_rows, list_width * rank_width, rhs_width)
        return jnp.einsum("ac,tcr->tar", stacked, flattened, preferred_element_type=jnp.float32)

    fields = lax.map(
        one_block,
        (sources.reshape(blocks, block_rows, list_width), counts.reshape(blocks, block_rows)),
    )
    return fields.reshape(target_rows, rank_width, rhs_width)


def shards(
    charges,
    basis_in,
    basis_out,
    transfer,
    leaf_coupling,
    parent_coupling,
    leaf_sources,
    leaf_counts,
    leaf_sends,
    parent_sources,
    parent_counts,
    parent_sends,
):
    per_dev = charges.shape[0]
    rank_width = basis_in.shape[1]
    rhs_width = charges.shape[2]
    parent_rows = transfer.shape[0]
    count_dev = lax.axis_size("leaf")
    own_index = lax.axis_index("leaf")
    up_leaf = jnp.einsum(
        "nkp,npr->nkr", basis_in, charges, preferred_element_type=jnp.float32
    ).astype(jnp.bfloat16)
    left_dev = jnp.maximum(own_index - 1, 0)
    right_dev = jnp.minimum(own_index + 1, count_dev - 1)
    padded = extended_2(up_leaf, (("leaf", 0),), per_dev)
    left_list = lax.dynamic_index_in_dim(leaf_sends, left_dev, 0, keepdims=False)[1]
    right_list = lax.dynamic_index_in_dim(leaf_sends, right_dev, 0, keepdims=False)[0]
    from_left = padded[:per_dev][left_list]
    from_right = padded[2 * per_dev :][right_list]
    leaf_rows_pool = jnp.concatenate([up_leaf, from_left, from_right], 0)
    leaf_field = pooled_product(leaf_rows_pool, leaf_sources, leaf_counts, leaf_coupling)
    grouped = up_leaf.reshape(parent_rows, 8, rank_width, rhs_width)
    up_parent = jnp.einsum(
        "pcab,pcar->pbr", transfer, grouped, preferred_element_type=jnp.float32
    ).astype(jnp.bfloat16)
    own_row = lax.dynamic_index_in_dim(parent_sends, own_index, 0, keepdims=False)
    arrived = lax.all_to_all(up_parent[own_row], "leaf", split_axis=0, concat_axis=0, tiled=True)
    parent_rows_pool = jnp.concatenate([up_parent, arrived], 0)
    parent_field = pooled_product(parent_rows_pool, parent_sources, parent_counts, parent_coupling)
    parent_down = parent_field.astype(jnp.bfloat16)
    pushed = jnp.einsum("pcab,pbr->pcar", transfer, parent_down, preferred_element_type=jnp.float32)
    leaf_total = (leaf_field + pushed.reshape(per_dev, rank_width, rhs_width)).astype(jnp.bfloat16)
    return jnp.einsum(
        "nkp,nkr->npr", basis_out, leaf_total, preferred_element_type=jnp.float32
    ).astype(jnp.bfloat16)


def solution(mesh):
    return jax.shard_map(
        shards,
        mesh=mesh,
        in_specs=(
            P("leaf", None, None),
            P("leaf", None, None),
            P("leaf", None, None),
            P("leaf", None, None, None),
            P(),
            P(),
            P("leaf", None),
            P("leaf"),
            P(),
            P("leaf", None),
            P("leaf"),
            P(),
        ),
        out_specs=P("leaf", None, None),
        check_vma=False,
    )
```

profile of v0, /device:TPU:2, one launch (start us, length us, event | category | flops | bytes accessed | tf_op | source)
XLA Modules:
  0.0 413.2 jit_solution(6113798593172714459)
XLA Ops:
  0.0 9.0 %convolution_convert_fusion = bf16[256,64,128]{2,1,0:T(8,128)(2,1)} fusion(bf16[256,64,128]{2,1,0:T(8,128)(2,1)} %param.15, bf16[256,128,128]{2,1,0:T(8,128)(2,1)} %param.14), kind=kOutput, calls=%fused_computation.18 | convolution fusion | flops 538968064 | bytes 16777216 | tf_op jit(solution)/shard_map/nkp,npr->nkr/dot_general | solution.py:69
  24.5 8.4 %all-to-all-start = ((bf16[128,64,128]{2,1,0:T(8,128)(2,1)}), bf16[128,64,128]{2,1,0:T(8,128)(2,1)S(1)}, u32[]{:S(2)}, u32[]{:S(2)}) async-start(bf16[128,64,128]{2,1,0:T(8,128)(2,1)} %gather_fusion.3), calls=%async_computation | async-start | bytes 4194304 | tf_op jit(solution)/shard_map/all_to_all | solution.py:86
  38.8 62.0 %all-to-all-done = bf16[128,64,128]{2,1,0:T(8,128)(2,1)S(1)} async-done(((bf16[128,64,128]{2,1,0:T(8,128)(2,1)}), bf16[128,64,128]{2,1,0:T(8,128)(2,1)S(1)}, u32[]{:S(2)}, u32[]{:S(2)}) %all-to-all-start) | async-done | bytes 2097184 | tf_op jit(solution)/shard_map/all_to_all | solution.py:86
  104.7 13.6 %gather_fusion.4 = bf16[512,64,128]{2,1,0:T(8,128)(2,1)} fusion(bf16[161,64,128]{2,1,0:T(8,128)(2,1)S(1)} %pad_maximum_fusion.1, s32[1024]{0:T(1024)} %pad_clamp_fusion.1), kind=kCustom, calls=%fused_computation.4 | custom fusion | bytes 16779264 | tf_op jit(solution)/shard_map/while/body/eval_jaxpr/gather | solution.py:38
  118.3 10.5 %fusion.7 = f32[32,128,8,64]{1,3,2,0:T(8,128)} fusion(bf16[32,8,64,64]{3,2,1,0:T(8,128)(2,1)} %param.17, bf16[32,16,64,128]{3,2,1,0:T(8,128)(2,1)} %bitcast.100, bf16[16,64,64]{2,1,0:T(8,128)(2,1)S(1)} %copy-done), kind=kOutput, calls=%fused_computation.25 | convolution fusion | flops 805568512 | bytes 19005440 | tf_op jit(solution)/shard_map/pcab,pbr->pcar/dot_general | solution.py:90
  136.6 7.0 %pad_maximum_fusion = bf16[513,64,128]{2,1,0:T(8,128)(2,1)} fusion(bf16[1,64,128]{2,1,0:T(8,128)(2,1)S(1)} %copy-done.5, bf16[128,64,128]{2,1,0:T(8,128)(2,1)} %gather_fusion.2, bf16[128,64,128]{2,1,0:T(8,128)(2,1)S(1)} %gather_fusion.1, bf16[256,64,128]{2,1,0:T(8,128)(2,1)} %convolution_convert_fusion), kind=kLoop, calls=%fused_computation.14 | loop fusion | flops 12607488 | bytes 16809984 | tf_op jit(solution)/shard_map/concatenate | solution.py:27
  143.6 241.8 %while.2 = (s32[]{:T(128)}, f32[8,32,64,128]{3,2,1,0:T(8,128)}, s32[8,32]{1,0:T(8,128)}, s32[8,32,16]{2,1,0:T(8,128)}, bf16[513,64,128]{2,1,0:T(8,128)(2,1)}, /*index=5*/bf16[64,1024]{1,0:T(8,128)(2,1)S(1)}, s32[]{:T(128)}) while((s32[]{:T(128)}, f32[8,32,64,128]{3,2,1,0:T(8,128)}, s32[8,32]{1,0:T(8,128)}, s32[8,32,16]{2,1,0:T(8,128)}, ...), condition=%wide.region_1.2_spmd, body=%wide.region_0.1_spmd.sunk | while | flops 536874496 | bytes 26362836 | solution.py:42
  145.2 22.7 %gather_fusion = bf16[512,64,128]{2,1,0:T(8,128)(2,1)} fusion(bf16[513,64,128]{2,1,0:T(8,128)(2,1)} %get-tuple-element.131, s32[1024]{0:T(1024)S(1)} %pad_clamp_fusion.6), kind=kCustom, calls=%fused_computation.clone.1 | custom fusion | bytes 16779264 | tf_op jit(solution)/shard_map/while/body/eval_jaxpr/gather | solution.py:38
  167.9 5.9 %fusion.31 = f32[8,32,64,128]{3,2,1,0:T(8,128)} fusion(f32[8,32,64,128]{3,2,1,0:T(8,128)} %get-tuple-element.121, s32[]{:T(128)} %get-tuple-element.120, bf16[32,1024,128]{2,1,0:T(8,128)(2,1)} %bitcast.99, bf16[64,1024]{1,0:T(8,128)(2,1)S(1)} %get-tuple-element.132), kind=kOutput, calls=%fused_computation.6.clone.1 | convolution fusion | flops 536870912 | bytes 9568768 | tf_op jit(solution)/shard_map/while/body/eval_jaxpr/ac,tcr->tar/dot_general | solution.py:40
  175.4 22.7 %gather_fusion = bf16[512,64,128]{2,1,0:T(8,128)(2,1)} fusion(bf16[513,64,128]{2,1,0:T(8,128)(2,1)} %get-tuple-element.131, s32[1024]{0:T(1024)S(1)} %pad_clamp_fusion.6), kind=kCustom, calls=%fused_computation.clone.1 | custom fusion | bytes 16779264 | tf_op jit(solution)/shard_map/while/body/eval_jaxpr/gather | solution.py:38
  198.2 5.9 %fusion.31 = f32[8,32,64,128]{3,2,1,0:T(8,128)} fusion(f32[8,32,64,128]{3,2,1,0:T(8,128)} %get-tuple-element.121, s32[]{:T(128)} %get-tuple-element.120, bf16[32,1024,128]{2,1,0:T(8,128)(2,1)} %bitcast.99, bf16[64,1024]{1,0:T(8,128)(2,1)S(1)} %get-tuple-element.132), kind=kOutput, calls=%fused_computation.6.clone.1 | convolution fusion | flops 536870912 | bytes 9568768 | tf_op jit(solution)/shard_map/while/body/eval_jaxpr/ac,tcr->tar/dot_general | solution.py:40
  205.7 22.7 %gather_fusion = bf16[512,64,128]{2,1,0:T(8,128)(2,1)} fusion(bf16[513,64,128]{2,1,0:T(8,128)(2,1)} %get-tuple-element.131, s32[1024]{0:T(1024)S(1)} %pad_clamp_fusion.6), kind=kCustom, calls=%fused_computation.clone.1 | custom fusion | bytes 16779264 | tf_op jit(solution)/shard_map/while/body/eval_jaxpr/gather | solution.py:38
  235.8 22.7 %gather_fusion = bf16[512,64,128]{2,1,0:T(8,128)(2,1)} fusion(bf16[513,64,128]{2,1,0:T(8,128)(2,1)} %get-tuple-element.131, s32[1024]{0:T(1024)S(1)} %pad_clamp_fusion.6), kind=kCustom, calls=%fused_computation.clone.1 | custom fusion | bytes 16779264 | tf_op jit(solution)/shard_map/while/body/eval_jaxpr/gather | solution.py:38
  258.6 5.9 %fusion.31 = f32[8,32,64,128]{3,2,1,0:T(8,128)} fusion(f32[8,32,64,128]{3,2,1,0:T(8,128)} %get-tuple-element.121, s32[]{:T(128)} %get-tuple-element.120, bf16[32,1024,128]{2,1,0:T(8,128)(2,1)} %bitcast.99, bf16[64,1024]{1,0:T(8,128)(2,1)S(1)} %get-tuple-element.132), kind=kOutput, calls=%fused_computation.6.clone.1 | convolution fusion | flops 536870912 | bytes 9568768 | tf_op jit(solution)/shard_map/while/body/eval_jaxpr/ac,tcr->tar/dot_general | solution.py:40
  266.1 22.7 %gather_fusion = bf16[512,64,128]{2,1,0:T(8,128)(2,1)} fusion(bf16[513,64,128]{2,1,0:T(8,128)(2,1)} %get-tuple-element.131, s32[1024]{0:T(1024)S(1)} %pad_clamp_fusion.6), kind=kCustom, calls=%fused_computation.clone.1 | custom fusion | bytes 16779264 | tf_op jit(solution)/shard_map/while/body/eval_jaxpr/gather | solution.py:38
  296.3 22.7 %gather_fusion = bf16[512,64,128]{2,1,0:T(8,128)(2,1)} fusion(bf16[513,64,128]{2,1,0:T(8,128)(2,1)} %get-tuple-element.131, s32[1024]{0:T(1024)S(1)} %pad_clamp_fusion.6), kind=kCustom, calls=%fused_computation.clone.1 | custom fusion | bytes 16779264 | tf_op jit(solution)/shard_map/while/body/eval_jaxpr/gather | solution.py:38
  319.0 6.0 %fusion.31 = f32[8,32,64,128]{3,2,1,0:T(8,128)} fusion(f32[8,32,64,128]{3,2,1,0:T(8,128)} %get-tuple-element.121, s32[]{:T(128)} %get-tuple-element.120, bf16[32,1024,128]{2,1,0:T(8,128)(2,1)} %bitcast.99, bf16[64,1024]{1,0:T(8,128)(2,1)S(1)} %get-tuple-element.132), kind=kOutput, calls=%fused_computation.6.clone.1 | convolution fusion | flops 536870912 | bytes 9568768 | tf_op jit(solution)/shard_map/while/body/eval_jaxpr/ac,tcr->tar/dot_general | solution.py:40
  326.5 22.8 %gather_fusion = bf16[512,64,128]{2,1,0:T(8,128)(2,1)} fusion(bf16[513,64,128]{2,1,0:T(8,128)(2,1)} %get-tuple-element.131, s32[1024]{0:T(1024)S(1)} %pad_clamp_fusion.6), kind=kCustom, calls=%fused_computation.clone.1 | custom fusion | bytes 16779264 | tf_op jit(solution)/shard_map/while/body/eval_jaxpr/gather | solution.py:38
  349.3 5.9 %fusion.31 = f32[8,32,64,128]{3,2,1,0:T(8,128)} fusion(f32[8,32,64,128]{3,2,1,0:T(8,128)} %get-tuple-element.121, s32[]{:T(128)} %get-tuple-element.120, bf16[32,1024,128]{2,1,0:T(8,128)(2,1)} %bitcast.99, bf16[64,1024]{1,0:T(8,128)(2,1)S(1)} %get-tuple-element.132), kind=kOutput, calls=%fused_computation.6.clone.1 | convolution fusion | flops 536870912 | bytes 9568768 | tf_op jit(solution)/shard_map/while/body/eval_jaxpr/ac,tcr->tar/dot_general | solution.py:40
  356.8 22.8 %gather_fusion = bf16[512,64,128]{2,1,0:T(8,128)(2,1)} fusion(bf16[513,64,128]{2,1,0:T(8,128)(2,1)} %get-tuple-element.131, s32[1024]{0:T(1024)S(1)} %pad_clamp_fusion.6), kind=kCustom, calls=%fused_computation.clone.1 | custom fusion | bytes 16779264 | tf_op jit(solution)/shard_map/while/body/eval_jaxpr/gather | solution.py:38
  379.5 6.0 %fusion.31 = f32[8,32,64,128]{3,2,1,0:T(8,128)} fusion(f32[8,32,64,128]{3,2,1,0:T(8,128)} %get-tuple-element.121, s32[]{:T(128)} %get-tuple-element.120, bf16[32,1024,128]{2,1,0:T(8,128)(2,1)} %bitcast.99, bf16[64,1024]{1,0:T(8,128)(2,1)S(1)} %get-tuple-element.132), kind=kOutput, calls=%fused_computation.6.clone.1 | convolution fusion | flops 536870912 | bytes 9568768 | tf_op jit(solution)/shard_map/while/body/eval_jaxpr/ac,tcr->tar/dot_general | solution.py:40
  385.5 7.9 %fusion.3 = bf16[256,64,128]{2,1,0:T(8,128)(2,1)S(1)} fusion(f32[32,128,8,64]{1,3,2,0:T(8,128)} %fusion.7, f32[8,32,64,128]{3,2,1,0:T(8,128)} %get-tuple-element.55), kind=kLoop, calls=%fused_computation.16 | loop fusion | flops 4194304 | bytes 20971520 | tf_op jit(solution)/shard_map/convert_element_type | solution.py:91
  393.4 7.9 %convert_bitcast_fusion = bf16[256,128,128]{1,2,0:T(8,128)(2,1)} fusion(bf16[256,64,128]{2,1,0:T(8,128)(2,1)S(1)} %fusion.3, bf16[256,64,128]{2,1,0:T(8,128)(2,1)} %param.16), kind=kOutput, calls=%fused_computation.17 | convolution fusion | flops 541065216 | bytes 16777216 | tf_op jit(solution)/shard_map/nkp,nkr->npr/dot_general | solution.py:92
  401.3 12.0 %copy.20 = bf16[256,128,128]{2,1,0:T(8,128)(2,1)} copy(bf16[256,128,128]{1,2,0:T(8,128)(2,1)} %convert_bitcast_fusion) | data formatting | bytes 16777216 | tf_op jit(solution)/shard_map/convert_element_type | solution.py:94
  (74 shorter events, 57.3 us)
Async XLA Ops:
  0.0 118.3 %copy-start = (bf16[16,64,64]{2,1,0:T(8,128)(2,1)S(1)}, bf16[16,64,64]{2,1,0:T(8,128)(2,1)}, u32[]{:S(2)}) copy-start(bf16[16,64,64]{2,1,0:T(8,128)(2,1)} %param.19) | copy-start | bytes 393220
  9.0 119.9 %collective-permute-start = (bf16[256,64,128]{2,1,0:T(8,128)(2,1)}, bf16[256,64,128]{2,1,0:T(8,128)(2,1)}, u32[]{:S(2)}, u32[]{:S(2)}) collective-permute-start(bf16[256,64,128]{2,1,0:T(8,128)(2,1)} %convolution_convert_fusion), channel_id=1, source_target_pairs={{0,1},{1,2},{2,3},{3,4},{4,5},{5,6},{6,7},{7,8},{8,9},{9,10},{10,1... | collective-permute-start | bytes 12582920 | tf_op jit(solution)/shard_map/ppermute | solution.py:16
  10.9 121.2 %collective-permute-start.1 = (bf16[256,64,128]{2,1,0:T(8,128)(2,1)}, bf16[256,64,128]{2,1,0:T(8,128)(2,1)}, u32[]{:S(2)}, u32[]{:S(2)}) collective-permute-start(bf16[256,64,128]{2,1,0:T(8,128)(2,1)} %convolution_convert_fusion), channel_id=1, source_target_pairs={{1,0},{2,1},{3,2},{4,3},{5,4},{6,5},{7,6},{8,7},{9,8},{10,9},{11,1... | collective-permute-start | bytes 12582920 | tf_op jit(solution)/shard_map/ppermute | solution.py:17
  22.4 10.6 %copy-start.3 = (bf16[16,64,64]{2,1,0:T(8,128)(2,1)S(1)}, bf16[16,64,64]{2,1,0:T(8,128)(2,1)}, u32[]{:S(2)}) copy-start(bf16[16,64,64]{2,1,0:T(8,128)(2,1)} %param.18) | copy-start | bytes 393220
  22.4 11.0 %copy-start.6 = (s32[256,16]{0,1:T(8,128)S(1)}, s32[256,16]{0,1:T(8,128)}, u32[]{:S(2)}) copy-start(s32[256,16]{0,1:T(8,128)} %param.20) | copy-start | bytes 49156
  24.5 76.3 %all-to-all-start = ((bf16[128,64,128]{2,1,0:T(8,128)(2,1)}), bf16[128,64,128]{2,1,0:T(8,128)(2,1)S(1)}, u32[]{:S(2)}, u32[]{:S(2)}) async-start(bf16[128,64,128]{2,1,0:T(8,128)(2,1)} %gather_fusion.3), calls=%async_computation | async-start | bytes 4194304 | tf_op jit(solution)/shard_map/all_to_all | solution.py:86
  100.9 1.3 copy-start.2
  102.2 0.6 copy-start.4
  128.9 7.7 %copy-start.5 = (bf16[1,64,128]{2,1,0:T(8,128)(2,1)S(1)}, bf16[1,64,128]{2,1,0:T(8,128)(2,1)}, u32[]{:S(2)}) copy-start(bf16[1,64,128]{2,1,0:T(8,128)(2,1)} %copy-done.4) | copy-start | bytes 49156
  401.3 12.0 %copy-start.1 = (bf16[16,64,64]{2,1,0:T(8,128)(2,1)S(1)}, bf16[16,64,64]{2,1,0:T(8,128)(2,1)}, u32[]{:S(2)}) copy-start(bf16[16,64,64]{2,1,0:T(8,128)(2,1)} %param.19) | copy-start | bytes 393220
where the time goes:
time: 415 us; the launch traced here: 413 us
  local copies, waits for them, and re-layouts  229 us (55%)
  matrix products  79.9 us (19%)
  waiting for transfers between devices  62 us (15%)
  other arithmetic  26.5 us (6%)
  starting transfers between devices  16.1 us (4%)
    gather x9, local copies, waits for them, and re-layouts, one_block(): gathered = extended[redirected]  195 us
    all_to_all x1, waiting for transfers between devices, shards(): lax.all_to_all(up_parent[own_row], 'leaf', split_axis=0, concat_axis=0, t...  62 us
    dot_general x8, matrix products, one_block(): jnp.einsum('ac,tcr->tar', stacked, flattened, preferred_element_type=jnp....  47.5 us
    convert_element_type x1, local copies, waits for them, and re-layouts, shards(): return jnp.einsum('nkp,nkr->npr', basis_out, leaf_total, preferred_elemen...  12 us
    dot_general x1, matrix products, shards(): jnp.einsum('pcab,pbr->pcar', transfer, parent_down, preferred_element_typ...  10.5 us
    dot_general x1, matrix products, shards(): jnp.einsum('nkp,npr->nkr', basis_in, charges, preferred_element_type=jnp....  8.98 us
    concatenate x2, other arithmetic, pooled_product(): jnp.concatenate([pool_rows, jnp.zeros((1, rank_width, rhs_width), pool_ro...  8.97 us
    all_to_all x1, starting transfers between devices, shards(): lax.all_to_all(up_parent[own_row], 'leaf', split_axis=0, concat_axis=0, t...  8.42 us
  transfers between devices with their start and end apart: 3, of which 1 were waited for; matrix products, arithmetic and copies ran while one was open for 10% of the time, Pallas kernels for 0%

commit v1 on v0

v1 whole, which is shorter than its diff:
```python
import functools

import jax
import jax.numpy as jnp
from jax import lax
from jax.experimental import pallas as pl
from jax.experimental.pallas import tpu as pltpu
from jax.sharding import PartitionSpec as P

MIB = 1 << 20
F32 = jnp.float32
BF16 = jnp.bfloat16


def params(mib):
    return pltpu.CompilerParams(
        vmem_limit_bytes=mib * MIB, dimension_semantics=("arbitrary",)
    )


def up_kernel(
    own_ref,
    leaf_sends_ref,
    parent_sends_ref,
    charges_ref,
    basis_ref,
    transfer_ref,
    up_leaf_ref,
    up_parent_ref,
    low_ref,
    high_ref,
    parents_ref,
    all_leaf,
):
    step = pl.program_id(0)
    steps = pl.num_programs(0)
    leaves = charges_ref.shape[0]
    rank, rhs = up_leaf_ref.shape[1:]
    for p in range(leaves // 8):
        for c in range(8):
            n = 8 * p + c
            up = jnp.dot(basis_ref[n], charges_ref[n], preferred_element_type=F32).astype(BF16)
            up_leaf_ref[n] = up
            all_leaf[step * leaves + n] = up
        stacked = transfer_ref[p].reshape(8 * rank, rank)
        below = up_leaf_ref[8 * p : 8 * p + 8].reshape(8 * rank, rhs)
        up_parent_ref[step * (leaves // 8) + p] = lax.dot_general(
            stacked, below, (((0,), (0,)), ((), ())), preferred_element_type=F32
        ).astype(BF16)

    @pl.when(step == steps - 1)
    def _():
        mine = lax.rem(own_ref[0], parent_sends_ref.shape[0])

        @pl.loop(0, low_ref.shape[0], unroll=4)
        def _(i):
            low_ref[i] = all_leaf[leaf_sends_ref[0, 0, i]]
            high_ref[i] = all_leaf[leaf_sends_ref[0, 1, i]]

        @pl.loop(0, parents_ref.shape[0], unroll=4)
        def _(i):
            parents_ref[i] = up_parent_ref[parent_sends_ref[mine, i]]


def upward(own, leaf_sends, parent_sends, charges, basis_in, transfer):
    per_dev, points, rhs = charges.shape
    rank = basis_in.shape[1]
    parents = transfer.shape[0]
    side = leaf_sends.shape[2]
    count_dev = parent_sends.shape[0]
    steps = 8
    lb = per_dev // steps
    whole = lambda i, own: (0, 0, 0)
    return pl.pallas_call(
        up_kernel,
        grid_spec=pltpu.PrefetchScalarGridSpec(
            num_scalar_prefetch=1,
            grid=(steps,),
            in_specs=[
                pl.BlockSpec((1, 2, side), lambda i, own: (own[0], 0, 0), memory_space=pltpu.SMEM),
                pl.BlockSpec((8, count_dev), lambda i, own: (own[0] // 8, 0), memory_space=pltpu.SMEM),
                pl.BlockSpec((lb, points, rhs), lambda i, own: (i, 0, 0)),
                pl.BlockSpec((lb, rank, points), lambda i, own: (i, 0, 0)),
                pl.BlockSpec((lb // 8, 8, rank, rank), lambda i, own: (i, 0, 0, 0)),
            ],
            out_specs=[
                pl.BlockSpec((lb, rank, rhs), lambda i, own: (i, 0, 0)),
                pl.BlockSpec((parents, rank, rhs), whole),
                pl.BlockSpec((side, rank, rhs), whole),
                pl.BlockSpec((side, rank, rhs), whole),
                pl.BlockSpec((count_dev, rank, rhs), whole),
            ],
            scratch_shapes=[pltpu.VMEM((per_dev, rank, rhs), BF16)],
        ),
        out_shape=[
            jax.ShapeDtypeStruct((per_dev, rank, rhs), BF16),
            jax.ShapeDtypeStruct((parents, rank, rhs), BF16),
            jax.ShapeDtypeStruct((side, rank, rhs), BF16),
            jax.ShapeDtypeStruct((side, rank, rhs), BF16),
            jax.ShapeDtypeStruct((count_dev, rank, rhs), BF16),
        ],
        compiler_params=params(48),
        name="upward",
    )(own, leaf_sends, parent_sends, charges, basis_in, transfer)


def gathered(pool, sources, counts, row, zero_row):
    width = sources.shape[1]
    count = counts[row]
    tiles = [pool[jnp.where(j < count, sources[row, j], zero_row)] for j in range(width)]
    return jnp.concatenate(tiles, axis=0)


def leaf_kernel(
    sources_ref,
    counts_ref,
    stacked_ref,
    own_ref,
    left_ref,
    right_ref,
    field_ref,
    pool,
    sems,
):
    step = pl.program_id(0)
    block = field_ref.shape[0]
    own_rows, rank, rhs = own_ref.shape
    left_rows = left_ref.shape[0]
    right_rows = right_ref.shape[0]
    zero_row = own_rows + left_rows + right_rows

    @pl.when(step == 0)
    def _():
        copies = [
            pltpu.make_async_copy(own_ref, pool.at[pl.ds(0, own_rows)], sems.at[0]),
            pltpu.make_async_copy(left_ref, pool.at[pl.ds(own_rows, left_rows)], sems.at[1]),
            pltpu.make_async_copy(right_ref, pool.at[pl.ds(own_rows + left_rows, right_rows)], sems.at[2]),
        ]
        for copy in copies:
            copy.start()
        pool[zero_row] = jnp.zeros((rank, rhs), BF16)
        for copy in copies:
            copy.wait()

    @pl.loop(0, block // 2)
    def _(i):
        row = step * block + 2 * i
        pair = jnp.concatenate(
            [
                gathered(pool, sources_ref, counts_ref, row, zero_row),
                gathered(pool, sources_ref, counts_ref, row + 1, zero_row),
            ],
            axis=1,
        )
        field = jnp.dot(stacked_ref[...], pair, preferred_element_type=F32)
        field_ref[2 * i] = field[:, :rhs].astype(field_ref.dtype)
        field_ref[2 * i + 1] = field[:, rhs:].astype(field_ref.dtype)


def leaf_lists(sources, counts, stacked, own, left, right):
    per_dev, rank, rhs = own.shape
    rows = own.shape[0] + left.shape[0] + right.shape[0]
    steps = 8
    block = per_dev // steps
    return pl.pallas_call(
        leaf_kernel,
        grid=(steps,),
        in_specs=[
            pl.BlockSpec(memory_space=pltpu.SMEM),
            pl.BlockSpec(memory_space=pltpu.SMEM),
            pl.BlockSpec(stacked.shape, lambda i: (0, 0)),
            pl.BlockSpec(memory_space=pl.ANY),
            pl.BlockSpec(memory_space=pl.ANY),
            pl.BlockSpec(memory_space=pl.ANY),
        ],
        out_specs=pl.BlockSpec((block, rank, rhs), lambda i: (i, 0, 0)),
        out_shape=jax.ShapeDtypeStruct((per_dev, rank, rhs), F32),
        scratch_shapes=[
            pltpu.VMEM((rows + 1, rank, rhs), BF16),
            pltpu.SemaphoreType.DMA((3,)),
        ],
        compiler_params=params(32),
        name="leaf_lists",
    )(sources, counts, stacked, own, left, right)


def down_kernel(
    sources_ref,
    counts_ref,
    stacked_ref,
    own_ref,
    arrived_ref,
    transfer_ref,
    field_ref,
    basis_ref,
    potential_ref,
    pool,
    sems,
):
    step = pl.program_id(0)
    block = transfer_ref.shape[0]
    own_rows, rank, rhs = own_ref.shape
    arrived_rows = arrived_ref.shape[0]
    zero_row = own_rows + arrived_rows

    @pl.when(step == 0)
    def _():
        copies = [
            pltpu.make_async_copy(own_ref, pool.at[pl.ds(0, own_rows)], sems.at[0]),
            pltpu.make_async_copy(arrived_ref, pool.at[pl.ds(own_rows, arrived_rows)], sems.at[1]),
        ]
        for copy in copies:
            copy.start()
        pool[zero_row] = jnp.zeros((rank, rhs), BF16)
        for copy in copies:
            copy.wait()

    for i in range(block // 2):
        row = step * block + 2 * i
        pair = jnp.concatenate(
            [
                gathered(pool, sources_ref, counts_ref, row, zero_row),
                gathered(pool, sources_ref, counts_ref, row + 1, zero_row),
            ],
            axis=1,
        )
        down = jnp.dot(stacked_ref[...], pair, preferred_element_type=F32).astype(BF16)
        for k in range(2):
            p = 2 * i + k
            pushed = jnp.dot(
                transfer_ref[p].reshape(8 * rank, rank),
                down[:, k * rhs : (k + 1) * rhs],
                preferred_element_type=F32,
            )
            for c in range(8):
                n = 8 * p + c
                total = (field_ref[n] + pushed[c * rank : (c + 1) * rank]).astype(BF16)
                potential_ref[n] = lax.dot_general(
                    basis_ref[n], total, (((0,), (0,)), ((), ())), preferred_element_type=F32
                ).astype(BF16)


def downward(sources, counts, stacked, own, arrived, transfer, field, basis_out):
    parents, rank, rhs = own.shape
    per_dev, _, points = basis_out.shape
    rows = own.shape[0] + arrived.shape[0]
    steps = 8
    block = parents // steps
    return pl.pallas_call(
        down_kernel,
        grid=(steps,),
        in_specs=[
            pl.BlockSpec(memory_space=pltpu.SMEM),
            pl.BlockSpec(memory_space=pltpu.SMEM),
            pl.BlockSpec(stacked.shape, lambda i: (0, 0)),
            pl.BlockSpec(memory_space=pl.ANY),
            pl.BlockSpec(memory_space=pl.ANY),
            pl.BlockSpec((block, 8, rank, rank), lambda i: (i, 0, 0, 0)),
            pl.BlockSpec((8 * block, rank, rhs), lambda i: (i, 0, 0)),
            pl.BlockSpec((8 * block, rank, points), lambda i: (i, 0, 0)),
        ],
        out_specs=pl.BlockSpec((8 * block, points, rhs), lambda i: (i, 0, 0)),
        out_shape=jax.ShapeDtypeStruct((per_dev, points, rhs), BF16),
        scratch_shapes=[
            pltpu.VMEM((rows + 1, rank, rhs), BF16),
            pltpu.SemaphoreType.DMA((2,)),
        ],
        compiler_params=params(32),
        name="downward",
    )(sources, counts, stacked, own, arrived, transfer, field, basis_out)


def side_by_side(coupling):
    width, rank, inner = coupling.shape
    return jnp.transpose(coupling, (1, 0, 2)).reshape(rank, width * inner)


def shards(
    charges,
    basis_in,
    basis_out,
    transfer,
    leaf_coupling,
    parent_coupling,
    leaf_sources,
    leaf_counts,
    leaf_sends,
    parent_sources,
    parent_counts,
    parent_sends,
):
    size = lax.axis_size("leaf")
    own = lax.axis_index("leaf").astype(jnp.int32).reshape(1)
    up = [(i, i + 1) for i in range(size - 1)]
    down = [(j, i) for i, j in up]
    up_leaf, up_parent, low, high, offered = upward(
        own, leaf_sends, parent_sends, charges, basis_in, transfer
    )
    from_left = lax.ppermute(high, "leaf", up)
    from_right = lax.ppermute(low, "leaf", down)
    arrived = lax.all_to_all(offered, "leaf", split_axis=0, concat_axis=0, tiled=True)
    field = leaf_lists(
        leaf_sources, leaf_counts, side_by_side(leaf_coupling), up_leaf, from_left, from_right
    )
    return downward(
        parent_sources,
        parent_counts,
        side_by_side(parent_coupling),
        up_parent,
        arrived,
        transfer,
        field,
        basis_out,
    )


def solution(mesh):
    return jax.shard_map(
        shards,
        mesh=mesh,
        in_specs=(
            P("leaf", None, None),
            P("leaf", None, None),
            P("leaf", None, None),
            P("leaf", None, None, None),
            P(),
            P(),
            P("leaf", None),
            P("leaf"),
            P(),
            P("leaf", None),
            P("leaf"),
            P(),
        ),
        out_specs=P("leaf", None, None),
        check_vma=False,
    )
```

time: 415 us -> 139 us (0.33)
  the two profiles are of different devices: /device:TPU:2 before, /device:TPU:5 now
where the time goes in v1:
time: 139 us; the launch traced here: 138 us
  Pallas kernels  63.7 us (46%)
  waiting for transfers between devices  41.6 us (30%)
  starting transfers between devices  16.5 us (12%)
  local copies, waits for them, and re-layouts  16 us (12%)
    pallas_call x1, Pallas kernels, leaf_lists(): pl.pallas_call(leaf_kernel, grid=(steps,), in_specs=[pl.BlockSpec(memory_...  32.9 us
    ppermute x1, waiting for transfers between devices, shards(): from_left = lax.ppermute(high, 'leaf', up)  27.9 us
    pallas_call x1, Pallas kernels, upward(): pl.pallas_call(up_kernel, grid_spec=pltpu.PrefetchScalarGridSpec(num_scal...  16.2 us
    unnamed x28, local copies, waits for them, and re-layouts  15.3 us
    pallas_call x1, Pallas kernels, downward(): pl.pallas_call(down_kernel, grid=(steps,), in_specs=[pl.BlockSpec(memory_...  14.6 us
    ppermute x1, waiting for transfers between devices, shards(): from_right = lax.ppermute(low, 'leaf', down)  13.7 us
    all_to_all x1, starting transfers between devices, shards(): lax.all_to_all(offered, 'leaf', split_axis=0, concat_axis=0, tiled=True)  10.4 us
    ppermute x1, starting transfers between devices, shards(): from_left = lax.ppermute(high, 'leaf', up)  4.24 us
  transfers between devices with their start and end apart: 3, of which 2 were waited for; matrix products, arithmetic and copies ran while one was open for 1% of the time, Pallas kernels for 24%

profile of v1, /device:TPU:5, one launch (start us, length us, event | category | flops | bytes accessed | tf_op | source)
XLA Modules:
  0.0 137.9 jit_solution(6567121702919446437)
XLA Ops:
  0.0 0.9 copy-done.5
  0.9 0.8 copy-done.6
  1.7 16.2 %upward.1 = (bf16[256,64,128]{2,1,0:T(8,128)(2,1)}, bf16[32,64,128]{2,1,0:T(8,128)(2,1)S(1)}, bf16[128,64,128]{2,1,0:T(8,128)(2,1)}, bf16[128,64,128]{2,1,0:T(8,128)(2,1)}, bf16[128,64,128]{2,1,0:T(8,128)(2,1)}) custom-call(s32[1]{0:T(128)} %bitcast.1.own_ref, s32[128,2,128]{2,1,0:T(2,128)S(1)} %copy-done.5, s32[128,128]{1,0:T(8,128)S(1)} %copy-done.6, ...), custom_call_target="tpu_custom_call" | custom-call | tf_op jit(solution)/shard_map/upward/pallas_call | solution.py:74
  17.9 0.0 copy-start.11
  18.0 0.0 copy-start.7
  18.0 4.2 %collective-permute-start = (bf16[128,64,128]{2,1,0:T(8,128)(2,1)}, bf16[128,64,128]{2,1,0:T(8,128)(2,1)}, u32[]{:S(2)}, u32[]{:S(2)}) collective-permute-start(bf16[128,64,128]{2,1,0:T(8,128)(2,1)} %get-tuple-element.13), channel_id=1, source_target_pairs={{0,1},{1,2},{2,3},{3,4},{4,5},{5,6},{6,7},{7,8},{8,9},{9,10},{10,1... | collective-permute-start | bytes 6291464 | tf_op jit(solution)/shard_map/ppermute | solution.py:299
  22.2 1.9 %collective-permute-start.1 = (bf16[128,64,128]{2,1,0:T(8,128)(2,1)}, bf16[128,64,128]{2,1,0:T(8,128)(2,1)}, u32[]{:S(2)}, u32[]{:S(2)}) collective-permute-start(bf16[128,64,128]{2,1,0:T(8,128)(2,1)} %get-tuple-element.14), channel_id=1, source_target_pairs={{1,0},{2,1},{3,2},{4,3},{5,4},{6,5},{7,6},{8,7},{9,8},{10,9},{11,1... | collective-permute-start | bytes 6291464 | tf_op jit(solution)/shard_map/ppermute | solution.py:300
  24.2 10.4 %all-to-all-start = ((bf16[128,64,128]{2,1,0:T(8,128)(2,1)}), bf16[128,64,128]{2,1,0:T(8,128)(2,1)S(1)}, u32[]{:S(2)}, u32[]{:S(2)}) async-start(bf16[128,64,128]{2,1,0:T(8,128)(2,1)} %get-tuple-element.11), calls=%async_computation | async-start | bytes 4194304 | tf_op jit(solution)/shard_map/all_to_all | solution.py:301
  34.5 0.2 copy.14
  34.7 0.2 reshape.11.stacked_ref
  34.9 0.1 copy.15.sources_ref
  35.0 0.2 copy.13
  35.2 0.2 reshape.9.stacked_ref
  35.4 0.1 copy.16.sources_ref
  35.5 27.9 %collective-permute-done.left_ref = bf16[128,64,128]{2,1,0:T(8,128)(2,1)} collective-permute-done((bf16[128,64,128]{2,1,0:T(8,128)(2,1)}, bf16[128,64,128]{2,1,0:T(8,128)(2,1)}, u32[]{:S(2)}, u32[]{:S(2)}) %collective-permute-start) | collective-permute-done | bytes 2097184 | tf_op jit(solution)/shard_map/ppermute | solution.py:299
  63.4 13.7 %collective-permute-done.1.right_ref = bf16[128,64,128]{2,1,0:T(8,128)(2,1)} collective-permute-done((bf16[128,64,128]{2,1,0:T(8,128)(2,1)}, bf16[128,64,128]{2,1,0:T(8,128)(2,1)}, u32[]{:S(2)}, u32[]{:S(2)}) %collective-permute-start.1) | collective-permute-done | bytes 2097184 | tf_op jit(solution)/shard_map/ppermute | solution.py:300
  77.1 2.2 %copy-done.4 = bf16[256,64,128]{2,1,0:T(8,128)(2,1)S(1)} copy-done((bf16[256,64,128]{2,1,0:T(8,128)(2,1)S(1)}, bf16[256,64,128]{2,1,0:T(8,128)(2,1)}, u32[]{:S(2)}) %copy-start.4) | copy-done | bytes 4194328
  79.3 32.9 %leaf_lists.1.field_ref = f32[256,64,128]{2,1,0:T(8,128)S(1)} custom-call(s32[256,16]{1,0:T(8,128)S(1)} %copy.15.sources_ref, s32[256]{0:T(256)S(1)} %copy-done.7, bf16[64,1024]{1,0:T(8,128)(2,1)S(1)} %reshape.11.stacked_ref, bf16[256,64,128]{2,1,0:T(8,128)(2,1)S(1)} %copy-done.4, bf16[128,64,128]{2,1,0:T(8,128)(2,1)} %collective-permute-done.left_ref, ...), custom_call_target="tpu_custom_call" | custom-call | tf_op jit(solution)/shard_map/leaf_lists/pallas_call | solution.py:165
  112.1 0.0 copy-start
  112.1 3.4 %copy-done = f32[256,64,128]{2,1,0:T(8,128)} copy-done((f32[256,64,128]{2,1,0:T(8,128)}, f32[256,64,128]{2,1,0:T(8,128)S(1)}, u32[]{:S(2)}) %copy-start) | copy-done | bytes 8388632
  115.5 3.4 %copy-done.1 = f32[256,64,128]{2,1,0:T(8,128)S(1)} copy-done((f32[256,64,128]{2,1,0:T(8,128)S(1)}, f32[256,64,128]{2,1,0:T(8,128)}, u32[]{:S(2)}) %copy-start.1) | copy-done | bytes 8388632
  118.9 2.2 %copy-done.2 = bf16[32,8,64,64]{3,2,1,0:T(8,128)(2,1)S(1)} copy-done((bf16[32,8,64,64]{3,2,1,0:T(8,128)(2,1)S(1)}, bf16[32,8,64,64]{3,2,1,0:T(8,128)(2,1)}, u32[]{:S(2)}) %copy-start.2) | copy-done | bytes 2097176
  121.1 2.2 %copy-done.3 = bf16[256,64,128]{2,1,0:T(8,128)(2,1)S(1)} copy-done((bf16[256,64,128]{2,1,0:T(8,128)(2,1)S(1)}, bf16[256,64,128]{2,1,0:T(8,128)(2,1)}, u32[]{:S(2)}) %copy-start.3) | copy-done | bytes 4194328
  123.3 14.6 %downward.1 = bf16[256,128,128]{2,1,0:T(8,128)(2,1)} custom-call(s32[32,16]{1,0:T(8,128)S(1)} %copy.16.sources_ref, s32[32]{0:T(128)S(1)} %copy-done.8, bf16[64,1024]{1,0:T(8,128)(2,1)S(1)} %reshape.9.stacked_ref, bf16[32,64,128]{2,1,0:T(8,128)(2,1)S(1)} %get-tuple-element.10.own_ref, bf16[128,64,128]{2,1,0:T(8,128)(2,1)S(1)} %all-to-all-done.arrived_ref, ...), custom_call_target="tpu_custom_call" | custom-call | tf_op jit(solution)/shard_map/downward/pallas_call | solution.py:249
  (17 shorter events, 0.0 us)
Async XLA Ops:
  0.0 0.9 copy-start.5
  0.9 0.8 copy-start.6
  17.9 16.6 %copy-start.9 = (bf16[16,64,64]{2,1,0:T(8,128)(2,1)S(1)}, bf16[16,64,64]{2,1,0:T(8,128)(2,1)}, u32[]{:S(2)}) copy-start(bf16[16,64,64]{2,1,0:T(8,128)(2,1)} %param.16) | copy-start | bytes 393220
  17.9 17.0 %copy-start.11 = (s32[256,16]{0,1:T(8,128)S(1)}, s32[256,16]{0,1:T(8,128)}, u32[]{:S(2)}) copy-start(s32[256,16]{0,1:T(8,128)} %param.18) | copy-start | bytes 49156
  17.9 17.1 %copy-start.10 = (bf16[16,64,64]{2,1,0:T(8,128)(2,1)S(1)}, bf16[16,64,64]{2,1,0:T(8,128)(2,1)}, u32[]{:S(2)}) copy-start(bf16[16,64,64]{2,1,0:T(8,128)(2,1)} %param.17) | copy-start | bytes 393220
  18.0 17.5 %copy-start.12 = (s32[32,16]{0,1:T(8,128)S(1)}, s32[32,16]{0,1:T(8,128)}, u32[]{:S(2)}) copy-start(s32[32,16]{0,1:T(8,128)} %param.21) | copy-start | bytes 6148
  18.0 59.1 %copy-start.7 = (s32[256]{0:T(256)S(1)}, s32[256]{0:T(256)}, u32[]{:S(2)}) copy-start(s32[256]{0:T(256)} %counts_ref.2) | copy-start | bytes 3076
  18.0 45.4 %collective-permute-start = (bf16[128,64,128]{2,1,0:T(8,128)(2,1)}, bf16[128,64,128]{2,1,0:T(8,128)(2,1)}, u32[]{:S(2)}, u32[]{:S(2)}) collective-permute-start(bf16[128,64,128]{2,1,0:T(8,128)(2,1)} %get-tuple-element.13), channel_id=1, source_target_pairs={{0,1},{1,2},{2,3},{3,4},{4,5},{5,6},{6,7},{7,8},{8,9},{9,10},{10,1... | collective-permute-start | bytes 6291464 | tf_op jit(solution)/shard_map/ppermute | solution.py:299
  22.2 54.8 %collective-permute-start.1 = (bf16[128,64,128]{2,1,0:T(8,128)(2,1)}, bf16[128,64,128]{2,1,0:T(8,128)(2,1)}, u32[]{:S(2)}, u32[]{:S(2)}) collective-permute-start(bf16[128,64,128]{2,1,0:T(8,128)(2,1)} %get-tuple-element.14), channel_id=1, source_target_pairs={{1,0},{2,1},{3,2},{4,3},{5,4},{6,5},{7,6},{8,7},{9,8},{10,9},{11,1... | collective-permute-start | bytes 6291464 | tf_op jit(solution)/shard_map/ppermute | solution.py:300
  24.2 91.4 %all-to-all-start = ((bf16[128,64,128]{2,1,0:T(8,128)(2,1)}), bf16[128,64,128]{2,1,0:T(8,128)(2,1)S(1)}, u32[]{:S(2)}, u32[]{:S(2)}) async-start(bf16[128,64,128]{2,1,0:T(8,128)(2,1)} %get-tuple-element.11), calls=%async_computation | async-start | bytes 4194304 | tf_op jit(solution)/shard_map/all_to_all | solution.py:301
  77.1 2.2 %copy-start.4 = (bf16[256,64,128]{2,1,0:T(8,128)(2,1)S(1)}, bf16[256,64,128]{2,1,0:T(8,128)(2,1)}, u32[]{:S(2)}) copy-start(bf16[256,64,128]{2,1,0:T(8,128)(2,1)} %get-tuple-element.12.own_ref) | copy-start | bytes 12582916
  79.3 36.3 %copy-start.8 = (s32[32]{0:T(128)S(1)}, s32[32]{0:T(128)}, u32[]{:S(2)}) copy-start(s32[32]{0:T(128)} %counts_ref.3) | copy-start | bytes 388
  112.1 3.4 %copy-start = (f32[256,64,128]{2,1,0:T(8,128)}, f32[256,64,128]{2,1,0:T(8,128)S(1)}, u32[]{:S(2)}) copy-start(f32[256,64,128]{2,1,0:T(8,128)S(1)} %leaf_lists.1.field_ref) | copy-start | bytes 25165828
  115.5 3.4 %copy-start.1 = (f32[256,64,128]{2,1,0:T(8,128)S(1)}, f32[256,64,128]{2,1,0:T(8,128)}, u32[]{:S(2)}) copy-start(f32[256,64,128]{2,1,0:T(8,128)} %copy-done) | copy-start | bytes 25165828
  118.9 2.2 %copy-start.2 = (bf16[32,8,64,64]{3,2,1,0:T(8,128)(2,1)S(1)}, bf16[32,8,64,64]{3,2,1,0:T(8,128)(2,1)}, u32[]{:S(2)}) copy-start(bf16[32,8,64,64]{3,2,1,0:T(8,128)(2,1)} %transfer_ref.3) | copy-start | bytes 6291460
  121.1 2.2 %copy-start.3 = (bf16[256,64,128]{2,1,0:T(8,128)(2,1)S(1)}, bf16[256,64,128]{2,1,0:T(8,128)(2,1)}, u32[]{:S(2)}) copy-start(bf16[256,64,128]{2,1,0:T(8,128)(2,1)} %basis_ref.3) | copy-start | bytes 12582916

commit v2 on v0

v2 whole, which is shorter than its diff:
```python
import jax
import jax.numpy as jnp
from jax import lax
from jax.experimental import pallas as pl
from jax.experimental.pallas import tpu as pltpu
from jax.sharding import PartitionSpec as P

MIB = 1 << 20
F32 = jnp.float32
BF16 = jnp.bfloat16

IN_VMEM = pl.BlockSpec(memory_space=pltpu.VMEM)
IN_SMEM = pl.BlockSpec(memory_space=pltpu.SMEM)
IN_HBM = pl.BlockSpec(memory_space=pltpu.HBM)


def params(mib):
    return pltpu.CompilerParams(vmem_limit_bytes=mib * MIB)


def cost(flops, moved):
    return pl.CostEstimate(flops=flops, bytes_accessed=moved, transcendentals=0)


def hbm(x):
    return pltpu.with_memory_space_constraint(x, pltpu.HBM)


def vmem(x):
    return pltpu.with_memory_space_constraint(x, pltpu.VMEM)


def first_rows_dot(a, b):
    return lax.dot_general(a, b, (((0,), (0,)), ((), ())), preferred_element_type=F32)


def leaves_kernel(
    own_ref, sends_ref, charges_hbm, basis_hbm, up_ref, low_ref, high_ref,
    charges, basis, sends, sems, send_sem,
):
    chunks = sems.shape[1]
    rows = charges.shape[0] // chunks

    def part(k, which):
        at = pl.ds(k * rows, rows)
        source, target = ((charges_hbm, charges), (basis_hbm, basis))[which]
        return pltpu.make_async_copy(source.at[at], target.at[at], sems.at[which, k])

    listing = pltpu.make_async_copy(sends_ref.at[own_ref[0]], sends, send_sem)
    for k in range(chunks):
        part(k, 0).start()
        part(k, 1).start()
    listing.start()
    for k in range(chunks):
        part(k, 0).wait()
        part(k, 1).wait()

        @pl.loop(0, rows // UP_LEAVES)
        def _(i):
            for c in range(UP_LEAVES):
                n = k * rows + UP_LEAVES * i + c
                up_ref[n] = jnp.dot(basis[n], charges[n], preferred_element_type=F32).astype(BF16)

    listing.wait()

    @pl.loop(0, low_ref.shape[0] // 4)
    def _(i):
        for c in range(4):
            low_ref[4 * i + c] = up_ref[sends[0, 4 * i + c]]
            high_ref[4 * i + c] = up_ref[sends[1, 4 * i + c]]


UP_LEAVES = 32


def leaf_coefficients(own, leaf_sends, charges, basis_in):
    per_dev, points, rhs = charges.shape
    rank = basis_in.shape[1]
    side = leaf_sends.shape[2]
    chunks = 8
    return pl.pallas_call(
        leaves_kernel,
        in_specs=[IN_SMEM, IN_HBM, IN_HBM, IN_HBM],
        out_specs=[IN_VMEM] * 3,
        out_shape=[
            pltpu.VMEM((per_dev, rank, rhs), BF16),
            pltpu.VMEM((side, rank, rhs), BF16),
            pltpu.VMEM((side, rank, rhs), BF16),
        ],
        scratch_shapes=[
            pltpu.VMEM((per_dev, points, rhs), BF16),
            pltpu.VMEM((per_dev, rank, points), BF16),
            pltpu.SMEM((2, side), jnp.int32),
            pltpu.SemaphoreType.DMA((2, chunks)),
            pltpu.SemaphoreType.DMA,
        ],
        compiler_params=params(16),
        cost_estimate=cost(2 * per_dev * rank * points * rhs, 20 * MIB),
        name="leaf_coefficients",
    )(own, hbm(leaf_sends), hbm(charges), hbm(basis_in))


def parents_kernel(
    own_ref, sends_ref, transfer_hbm, basis_hbm, leaf_ref, up_ref, offered_hbm, joined_hbm,
    transfer, basis, offered, joined, sends, sems, out_sems, send_sem, offer_sem,
):
    chunks = sems.shape[1]
    parents, _, rank, _ = transfer.shape
    rhs = leaf_ref.shape[2]
    rows = parents // chunks

    def part(k, which):
        if which:
            at = pl.ds(8 * k * rows, 8 * rows)
            return pltpu.make_async_copy(basis_hbm.at[at], basis.at[at], sems.at[1, k])
        at = pl.ds(k * rows, rows)
        return pltpu.make_async_copy(transfer_hbm.at[at], transfer.at[at], sems.at[0, k])

    def result(k):
        at = pl.ds(8 * k * rows, 8 * rows)
        return pltpu.make_async_copy(joined.at[at], joined_hbm.at[at], out_sems.at[k])

    own = own_ref[0]
    first = pl.multiple_of((own // 8) * 8, 8)
    listing = pltpu.make_async_copy(sends_ref.at[pl.ds(first, 8)], sends, send_sem)
    for k in range(chunks):
        part(k, 0).start()
    listing.start()
    for k in range(chunks):
        part(k, 1).start()
    for k in range(chunks):
        part(k, 0).wait()

        @pl.loop(0, rows // 4)
        def _(i):
            for c in range(4):
                p = k * rows + 4 * i + c
                below = leaf_ref[pl.ds(8 * p, 8)].reshape(8 * rank, rhs)
                up_ref[p] = first_rows_dot(transfer[p].reshape(8 * rank, rank), below).astype(BF16)

    listing.wait()
    row = lax.rem(own, 8)

    @pl.loop(0, offered.shape[0] // 8)
    def _(i):
        for c in range(8):
            offered[8 * i + c] = up_ref[sends[row, 8 * i + c]]

    offer = pltpu.make_async_copy(offered, offered_hbm, offer_sem)
    offer.start()
    for k in range(chunks):
        part(k, 1).wait()

        @pl.loop(0, rows)
        def _(i):
            p = k * rows + i
            for c in range(8):
                n = 8 * p + c
                pushed = first_rows_dot(transfer[p, c], basis[n]).astype(BF16)
                joined[n] = jnp.concatenate([basis[n], pushed], axis=0).T

        result(k).start()
    offer.wait()
    for k in range(chunks):
        result(k).wait()


def parent_coefficients(own, parent_sends, transfer, basis_out, up_leaf):
    parents, _, rank, _ = transfer.shape
    per_dev, _, points = basis_out.shape
    rhs = up_leaf.shape[2]
    count_dev = parent_sends.shape[0]
    chunks = 4
    return pl.pallas_call(
        parents_kernel,
        in_specs=[IN_SMEM, IN_HBM, IN_HBM, IN_HBM, IN_VMEM],
        out_specs=[IN_VMEM, IN_HBM, IN_HBM],
        out_shape=[
            pltpu.VMEM((parents, rank, rhs), BF16),
            pltpu.HBM((count_dev, rank, rhs), BF16),
            pltpu.HBM((per_dev, points, 2 * rank), BF16),
        ],
        scratch_shapes=[
            pltpu.VMEM(transfer.shape, BF16),
            pltpu.VMEM(basis_out.shape, BF16),
            pltpu.VMEM((count_dev, rank, rhs), BF16),
            pltpu.VMEM((per_dev, points, 2 * rank), BF16),
            pltpu.SMEM((8, count_dev), jnp.int32),
            pltpu.SemaphoreType.DMA((2, chunks)),
            pltpu.SemaphoreType.DMA((chunks,)),
            pltpu.SemaphoreType.DMA,
            pltpu.SemaphoreType.DMA,
        ],
        compiler_params=params(24),
        cost_estimate=cost(32 * parents * rank * rank * rhs, 20 * MIB),
        name="parent_coefficients",
    )(own, hbm(parent_sends), hbm(transfer), hbm(basis_out), vmem(up_leaf))


def list_fields(sources_ref, stacked, pool, first, count):
    width = sources_ref.shape[0]
    tiles = [
        jnp.concatenate([pool[sources_ref[j, first + q]] for j in range(width)], axis=0)
        for q in range(count)
    ]
    return jnp.dot(stacked, jnp.concatenate(tiles, axis=1), preferred_element_type=F32)


def fill(pool, *parts):
    first = 0
    for part in parts:
        rows = part.shape[0]

        @pl.loop(0, rows // 8)
        def _(i):
            for c in range(8):
                pool[first + 8 * i + c] = part[8 * i + c]

        first += rows
    pool[first] = jnp.zeros(pool.shape[1:], pool.dtype)


def lists_kernel(sources_ref, stacked_ref, own_ref, left_ref, right_ref, field_hbm, pool, field, sems):
    chunks = sems.shape[0]
    own_rows, _, rhs = own_ref.shape
    rows = own_rows // chunks
    fill(pool, own_ref, left_ref, right_ref)

    def result(k):
        at = pl.ds(k * rows, rows)
        return pltpu.make_async_copy(field.at[at], field_hbm.at[at], sems.at[k])

    for k in range(chunks):

        @pl.loop(0, rows // LISTS)
        def _(i):
            first = k * rows + LISTS * i
            lists = list_fields(sources_ref, stacked_ref[...], pool, first, LISTS)
            for q in range(LISTS):
                field[first + q] = lists[:, q * rhs : (q + 1) * rhs].astype(BF16)

        result(k).start()
    for k in range(chunks):
        result(k).wait()


LISTS = 8


def leaf_lists(sources, stacked, own, left, right):
    per_dev, rank, rhs = own.shape
    rows = own.shape[0] + left.shape[0] + right.shape[0]
    return pl.pallas_call(
        lists_kernel,
        in_specs=[IN_SMEM, IN_VMEM, IN_VMEM, IN_VMEM, IN_VMEM],
        out_specs=IN_HBM,
        out_shape=pltpu.HBM((per_dev, rank, rhs), BF16),
        scratch_shapes=[
            pltpu.VMEM((rows + 1, rank, rhs), BF16),
            pltpu.VMEM((per_dev, rank, rhs), BF16),
            pltpu.SemaphoreType.DMA((4,)),
        ],
        compiler_params=params(20),
        cost_estimate=cost(2 * per_dev * sources.shape[0] * rank * rank * rhs, 12 * MIB),
        name="leaf_lists",
    )(sources, stacked, vmem(own), vmem(left), vmem(right))


def down_kernel(
    sources_ref, stacked_ref, own_ref, arrived_ref, field_hbm, joined_hbm, potential_hbm,
    pool, down, field, joined, potential, sems, out_sems,
):
    chunks = out_sems.shape[0]
    parents, _, rhs = own_ref.shape
    rows = joined.shape[0] // chunks

    def part(k, which):
        at = pl.ds(k * rows, rows)
        source, target = ((field_hbm, field), (joined_hbm, joined))[which]
        return pltpu.make_async_copy(source.at[at], target.at[at], sems.at[which, k])

    def result(k):
        at = pl.ds(k * rows, rows)
        return pltpu.make_async_copy(potential.at[at], potential_hbm.at[at], out_sems.at[k])

    for k in range(chunks):
        part(k, 0).start()
        part(k, 1).start()
    fill(pool, own_ref, arrived_ref)

    @pl.loop(0, parents // DOWN_LISTS)
    def _(i):
        lists = list_fields(sources_ref, stacked_ref[...], pool, DOWN_LISTS * i, DOWN_LISTS)
        for q in range(DOWN_LISTS):
            down[DOWN_LISTS * i + q] = lists[:, q * rhs : (q + 1) * rhs].astype(BF16)

    for k in range(chunks):
        part(k, 0).wait()
        part(k, 1).wait()

        @pl.loop(0, rows // (8 * DOWN_PARENTS))
        def _(i):
            for q in range(DOWN_PARENTS):
                p = k * (rows // 8) + DOWN_PARENTS * i + q
                for c in range(8):
                    n = 8 * p + c
                    both = jnp.concatenate([field[n], down[p]], axis=0)
                    potential[n] = jnp.dot(joined[n], both, preferred_element_type=F32).astype(BF16)

        result(k).start()
    for k in range(chunks):
        result(k).wait()


DOWN_LISTS = 8
DOWN_PARENTS = 4
DOWN_CHUNKS = 8


def downward(sources, stacked, own, arrived, field, joined):
    parents, rank, rhs = own.shape
    per_dev, points, _ = joined.shape
    rows = own.shape[0] + arrived.shape[0]
    chunks = DOWN_CHUNKS
    return pl.pallas_call(
        down_kernel,
        in_specs=[IN_SMEM, IN_VMEM, IN_VMEM, IN_VMEM, IN_HBM, IN_HBM],
        out_specs=IN_HBM,
        out_shape=pltpu.HBM((per_dev, points, rhs), BF16),
        scratch_shapes=[
            pltpu.VMEM((rows + 1, rank, rhs), BF16),
            pltpu.VMEM((parents, rank, rhs), BF16),
            pltpu.VMEM(field.shape, BF16),
            pltpu.VMEM(joined.shape, BF16),
            pltpu.VMEM((per_dev, points, rhs), BF16),
            pltpu.SemaphoreType.DMA((2, chunks)),
            pltpu.SemaphoreType.DMA((chunks,)),
        ],
        compiler_params=params(32),
        cost_estimate=cost(6 * per_dev * points * rank * rhs, 24 * MIB),
        name="downward",
    )(sources, stacked, vmem(own), vmem(arrived), hbm(field), hbm(joined))


def side_by_side(coupling):
    width, rank, inner = coupling.shape
    return jnp.transpose(coupling, (1, 0, 2)).reshape(rank, width * inner)


def used_slots(sources, counts, zero_row):
    slots = lax.broadcasted_iota(jnp.int32, sources.shape[::-1], 0)
    return jnp.where(slots < counts[None, :], sources.T, zero_row)


def shards(
    charges,
    basis_in,
    basis_out,
    transfer,
    leaf_coupling,
    parent_coupling,
    leaf_sources,
    leaf_counts,
    leaf_sends,
    parent_sources,
    parent_counts,
    parent_sends,
):
    size = lax.axis_size("leaf")
    own = lax.axis_index("leaf").astype(jnp.int32).reshape(1)
    up = [(i, i + 1) for i in range(size - 1)]
    down = [(j, i) for i, j in up]
    up_leaf, low, high = leaf_coefficients(own, leaf_sends, charges, basis_in)
    from_left = lax.ppermute(high, "leaf", up)
    from_right = lax.ppermute(low, "leaf", down)
    up_parent, offered, joined = parent_coefficients(
        own, parent_sends, transfer, basis_out, up_leaf
    )
    arrived = lax.all_to_all(offered, "leaf", split_axis=0, concat_axis=0, tiled=True)
    leaf_rows = up_leaf.shape[0] + low.shape[0] + high.shape[0]
    field = leaf_lists(
        used_slots(leaf_sources, leaf_counts, leaf_rows),
        side_by_side(leaf_coupling),
        up_leaf,
        from_left,
        from_right,
    )
    return downward(
        used_slots(parent_sources, parent_counts, up_parent.shape[0] + offered.shape[0]),
        side_by_side(parent_coupling),
        up_parent,
        arrived,
        field,
        joined,
    )


def solution(mesh):
    return jax.shard_map(
        shards,
        mesh=mesh,
        in_specs=(
            P("leaf", None, None),
            P("leaf", None, None),
            P("leaf", None, None),
            P("leaf", None, None, None),
            P(),
            P(),
            P("leaf", None),
            P("leaf"),
            P(),
            P("leaf", None),
            P("leaf"),
            P(),
        ),
        out_specs=P("leaf", None, None),
        check_vma=False,
    )
```

time: 415 us -> 79.7 us (0.19)
  local copies, waits for them, and re-layouts: 229 us -> 2.97 us
  matrix products: 79.9 us -> 0 us
  waiting for transfers between devices: 62 us -> 7.57 us
  Pallas kernels: 0 us -> 51.6 us
  other arithmetic: 26.5 us -> 0.01 us
    gather x12 -> x0, local copies, waits for them, and re-layouts: 205 us -> none  [the longest x9 195 us: one_block(): gathered = extended[redirected]]
    dot_general x12 -> x0, matrix products: 79.9 us -> none  [the longest x8 47.5 us: one_block(): jnp.einsum('ac,tcr->tar', stacked, flattened, preferred_element_type=jnp....]
    all_to_all x1, waiting for transfers between devices: 62 us -> 7.57 us  [shards(): lax.all_to_all(offered, 'leaf', split_axis=0, concat_axis=0, tiled=True)]
    pallas_call x0 -> x4, Pallas kernels: none -> 51.6 us  [the longest x1 19.6 us: leaf_lists(): pl.pallas_call(lists_kernel, in_specs=[IN_SMEM, IN_VMEM, IN_VMEM, IN_VMEM...]
    convert_element_type x1 -> x0, local copies, waits for them, and re-layouts: 12 us -> none  [shards(): return jnp.einsum('nkp,nkr->npr', basis_out, leaf_total, preferred_elemen...]
    concatenate x2 -> x0, other arithmetic: 8.97 us -> none  [pooled_product(): jnp.concatenate([pool_rows, jnp.zeros((1, rank_width, rhs_width), pool_ro...]
    convert_element_type x1 -> x0, other arithmetic: 7.94 us -> none  [shards(): (leaf_field + pushed.reshape(per_dev, rank_width, rhs_width)).astype(jnp....]
    select_n x12 -> x2, other arithmetic: 7.72 us -> 0.01 us  [used_slots(): return jnp.where(slots < counts[None, :], sources.T, zero_row)]
  transfers between devices with their start and end apart: 3 -> 3, of which waited for: 1 -> 1; matrix products, arithmetic and copies ran while one was open for 10% -> 1% of each run, Pallas kernels for 0% -> 44%
where the time goes in v2:
time: 79.7 us; the launch traced here: 78.5 us
  Pallas kernels  51.6 us (65%)
  starting transfers between devices  16.1 us (20%)
  waiting for transfers between devices  7.57 us (9%)
  local copies, waits for them, and re-layouts  2.97 us (4%)
    pallas_call x1, Pallas kernels, leaf_lists(): pl.pallas_call(lists_kernel, in_specs=[IN_SMEM, IN_VMEM, IN_VMEM, IN_VMEM...  19.6 us
    pallas_call x1, Pallas kernels, parent_coefficients(): pl.pallas_call(parents_kernel, in_specs=[IN_SMEM, IN_HBM, IN_HBM, IN_HBM,...  15.3 us
    pallas_call x1, Pallas kernels, downward(): pl.pallas_call(down_kernel, in_specs=[IN_SMEM, IN_VMEM, IN_VMEM, IN_VMEM,...  9.09 us
    all_to_all x1, starting transfers between devices, shards(): lax.all_to_all(offered, 'leaf', split_axis=0, concat_axis=0, tiled=True)  8.43 us
    pallas_call x1, Pallas kernels, leaf_coefficients(): pl.pallas_call(leaves_kernel, in_specs=[IN_SMEM, IN_HBM, IN_HBM, IN_HBM],...  7.68 us
    all_to_all x1, waiting for transfers between devices, shards(): lax.all_to_all(offered, 'leaf', split_axis=0, concat_axis=0, tiled=True)  7.57 us
    ppermute x1, starting transfers between devices, shards(): from_right = lax.ppermute(low, 'leaf', down)  5.75 us
    unnamed x16, local copies, waits for them, and re-layouts  2.23 us
  transfers between devices with their start and end apart: 3, of which 1 were waited for; matrix products, arithmetic and copies ran while one was open for 1% of the time, Pallas kernels for 44%

profile of v2, /device:TPU:2, one launch (start us, length us, event | category | flops | bytes accessed | tf_op | source)
XLA Modules:
  0.0 78.5 jit_solution(15391269909219104561)
XLA Ops:
  0.0 7.7 %leaf_coefficients.1 = (bf16[256,64,128]{2,1,0:T(8,128)(2,1)S(1)}, bf16[128,64,128]{2,1,0:T(8,128)(2,1)}, bf16[128,64,128]{2,1,0:T(8,128)(2,1)}) custom-call(s32[1]{0:T(128)} %bitcast.2.own_ref, s32[128,2,128]{2,1,0:T(2,128)} %sends_ref.2, bf16[256,128,128]{2,1,0:T(8,128)(2,1)} %charges_hbm.1, bf16[256,64,128]{2,1,0:T(8,128)(2,1)} %basis_hbm.2), custom_call_target="tpu_custom_call" | custom-call | flops 536870912 | bytes 20971520 | tf_op jit(solution)/shard_map/leaf_coefficients/pallas_call | solution.py:81
  7.7 0.0 copy-start
  7.7 1.9 %collective-permute-start = (bf16[128,64,128]{2,1,0:T(8,128)(2,1)}, bf16[128,64,128]{2,1,0:T(8,128)(2,1)}, u32[]{:S(2)}, u32[]{:S(2)}) collective-permute-start(bf16[128,64,128]{2,1,0:T(8,128)(2,1)} %get-tuple-element.14), channel_id=1, source_target_pairs={{0,1},{1,2},{2,3},{3,4},{4,5},{5,6},{6,7},{7,8},{8,9},{9,10},{10,1... | collective-permute-start | bytes 6291464 | tf_op jit(solution)/shard_map/ppermute | solution.py:374
  9.6 5.8 %collective-permute-start.1 = (bf16[128,64,128]{2,1,0:T(8,128)(2,1)}, bf16[128,64,128]{2,1,0:T(8,128)(2,1)}, u32[]{:S(2)}, u32[]{:S(2)}) collective-permute-start(bf16[128,64,128]{2,1,0:T(8,128)(2,1)} %get-tuple-element.15), channel_id=1, source_target_pairs={{1,0},{2,1},{3,2},{4,3},{5,4},{6,5},{7,6},{8,7},{9,8},{10,9},{11,1... | collective-permute-start | bytes 6291464 | tf_op jit(solution)/shard_map/ppermute | solution.py:375
  15.4 15.3 %parent_coefficients.1 = (bf16[32,64,128]{2,1,0:T(8,128)(2,1)S(1)}, bf16[128,64,128]{2,1,0:T(8,128)(2,1)}, bf16[256,128,128]{2,1,0:T(8,128)(2,1)}) custom-call(s32[1]{0:T(128)} %bitcast.2.own_ref, s32[128,128]{1,0:T(8,128)} %sends_ref.3, bf16[32,8,64,64]{3,2,1,0:T(8,128)(2,1)} %transfer_hbm.1, bf16[256,64,128]{2,1,0:T(8,128)(2,1)} %basis_hbm.3, ...), custom_call_target="tpu_custom_call" | custom-call | flops 536870912 | bytes 20971520 | tf_op jit(solution)/shard_map/parent_coefficients/pallas_call | solution.py:174
  30.7 0.0 copy-done
  30.7 0.0 copy-start.2
  30.7 0.0 copy-start.3
  30.7 0.0 copy-start.5
  30.7 0.0 copy-start.7
  30.7 0.0 copy-start.4
  30.7 0.0 copy-start.6
  30.7 8.4 %all-to-all-start = ((bf16[128,64,128]{2,1,0:T(8,128)(2,1)}), bf16[128,64,128]{2,1,0:T(8,128)(2,1)S(1)}, u32[]{:S(2)}, u32[]{:S(2)}) async-start(bf16[128,64,128]{2,1,0:T(8,128)(2,1)} %get-tuple-element.13), calls=%async_computation | async-start | bytes 4194304 | tf_op jit(solution)/shard_map/all_to_all | solution.py:379
  39.2 0.2 copy.14
  39.4 0.2 reshape.13.stacked_ref
  39.6 0.2 copy.13
  39.8 0.2 reshape.11.stacked_ref
  40.0 0.0 collective-permute-done.left_ref
  40.0 0.0 collective-permute-done.1.right_ref
  40.0 0.0 copy-start.1
  40.1 2.2 %copy-done.1 = bf16[256,64,128]{2,1,0:T(8,128)(2,1)S(1)} copy-done((bf16[256,64,128]{2,1,0:T(8,128)(2,1)S(1)}, bf16[256,64,128]{2,1,0:T(8,128)(2,1)}, u32[]{:S(2)}) %copy-start.1) | copy-done | bytes 4194328
  42.2 19.6 %leaf_lists.1.field_hbm = bf16[256,64,128]{2,1,0:T(8,128)(2,1)} custom-call(s32[16,256]{1,0:T(8,128)S(1)} %bitcast_select_fusion.sources_ref, bf16[64,1024]{1,0:T(8,128)(2,1)S(1)} %reshape.13.stacked_ref, bf16[256,64,128]{2,1,0:T(8,128)(2,1)S(1)} %copy-done.1, bf16[128,64,128]{2,1,0:T(8,128)(2,1)} %collective-permute-done.left_ref, ...), custom_call_target="tpu_custom_call" | custom-call | flops 4294967296 | bytes 12582912 | tf_op jit(solution)/shard_map/leaf_lists/pallas_call | solution.py:253
  61.8 7.6 %all-to-all-done.arrived_ref = bf16[128,64,128]{2,1,0:T(8,128)(2,1)S(1)} async-done(((bf16[128,64,128]{2,1,0:T(8,128)(2,1)}), bf16[128,64,128]{2,1,0:T(8,128)(2,1)S(1)}, u32[]{:S(2)}, u32[]{:S(2)}) %all-to-all-start) | async-done | bytes 2097184 | tf_op jit(solution)/shard_map/all_to_all | solution.py:379
  69.4 9.1 %downward.1 = bf16[256,128,128]{2,1,0:T(8,128)(2,1)} custom-call(s32[16,32]{1,0:T(8,128)S(1)} %bitcast_select_fusion.1.sources_ref, bf16[64,1024]{1,0:T(8,128)(2,1)S(1)} %reshape.11.stacked_ref, bf16[32,64,128]{2,1,0:T(8,128)(2,1)S(1)} %get-tuple-element.12.own_ref, bf16[128,64,128]{2,1,0:T(8,128)(2,1)S(1)} %all-to-all-done.arrived_ref, ...), custom_call_target="tpu_custom_call" | custom-call | flops 1610612736 | bytes 25165824 | tf_op jit(solution)/shard_map/downward/pallas_call | solution.py:325
  (8 shorter events, 0.0 us)
Async XLA Ops:
  7.7 23.0 %copy-start = (bf16[256,64,128]{2,1,0:T(8,128)(2,1)}, bf16[256,64,128]{2,1,0:T(8,128)(2,1)S(1)}, u32[]{:S(2)}) copy-start(bf16[256,64,128]{2,1,0:T(8,128)(2,1)S(1)} %get-tuple-element.11.leaf_ref.own_ref) | copy-start | bytes 12582916
  7.7 32.3 %collective-permute-start = (bf16[128,64,128]{2,1,0:T(8,128)(2,1)}, bf16[128,64,128]{2,1,0:T(8,128)(2,1)}, u32[]{:S(2)}, u32[]{:S(2)}) collective-permute-start(bf16[128,64,128]{2,1,0:T(8,128)(2,1)} %get-tuple-element.14), channel_id=1, source_target_pairs={{0,1},{1,2},{2,3},{3,4},{4,5},{5,6},{6,7},{7,8},{8,9},{9,10},{10,1... | collective-permute-start | bytes 6291464 | tf_op jit(solution)/shard_map/ppermute | solution.py:374
  9.6 30.4 %collective-permute-start.1 = (bf16[128,64,128]{2,1,0:T(8,128)(2,1)}, bf16[128,64,128]{2,1,0:T(8,128)(2,1)}, u32[]{:S(2)}, u32[]{:S(2)}) collective-permute-start(bf16[128,64,128]{2,1,0:T(8,128)(2,1)} %get-tuple-element.15), channel_id=1, source_target_pairs={{1,0},{2,1},{3,2},{4,3},{5,4},{6,5},{7,6},{8,7},{9,8},{10,9},{11,1... | collective-permute-start | bytes 6291464 | tf_op jit(solution)/shard_map/ppermute | solution.py:375
  30.7 8.5 %copy-start.2 = (bf16[16,64,64]{2,1,0:T(8,128)(2,1)S(1)}, bf16[16,64,64]{2,1,0:T(8,128)(2,1)}, u32[]{:S(2)}) copy-start(bf16[16,64,64]{2,1,0:T(8,128)(2,1)} %param.16) | copy-start | bytes 393220
  30.7 8.9 %copy-start.3 = (bf16[16,64,64]{2,1,0:T(8,128)(2,1)S(1)}, bf16[16,64,64]{2,1,0:T(8,128)(2,1)}, u32[]{:S(2)}) copy-start(bf16[16,64,64]{2,1,0:T(8,128)(2,1)} %param.17) | copy-start | bytes 393220
  30.7 9.3 %copy-start.5 = (s32[32,16]{0,1:T(8,128)S(1)}, s32[32,16]{0,1:T(8,128)}, u32[]{:S(2)}) copy-start(s32[32,16]{0,1:T(8,128)} %param.21) | copy-start | bytes 6148
  30.7 9.3 %copy-start.7 = (s32[32]{0:T(128)S(1)}, s32[32]{0:T(128)}, u32[]{:S(2)}) copy-start(s32[32]{0:T(128)} %param.22) | copy-start | bytes 388
  30.7 9.3 %copy-start.4 = (s32[256,16]{0,1:T(8,128)S(1)}, s32[256,16]{0,1:T(8,128)}, u32[]{:S(2)}) copy-start(s32[256,16]{0,1:T(8,128)} %param.18) | copy-start | bytes 49156
  30.7 9.3 %copy-start.6 = (s32[256]{0:T(256)S(1)}, s32[256]{0:T(256)}, u32[]{:S(2)}) copy-start(s32[256]{0:T(256)} %param.19) | copy-start | bytes 3076
  30.7 38.7 %all-to-all-start = ((bf16[128,64,128]{2,1,0:T(8,128)(2,1)}), bf16[128,64,128]{2,1,0:T(8,128)(2,1)S(1)}, u32[]{:S(2)}, u32[]{:S(2)}) async-start(bf16[128,64,128]{2,1,0:T(8,128)(2,1)} %get-tuple-element.13), calls=%async_computation | async-start | bytes 4194304 | tf_op jit(solution)/shard_map/all_to_all | solution.py:379
  40.0 2.2 %copy-start.1 = (bf16[256,64,128]{2,1,0:T(8,128)(2,1)S(1)}, bf16[256,64,128]{2,1,0:T(8,128)(2,1)}, u32[]{:S(2)}) copy-start(bf16[256,64,128]{2,1,0:T(8,128)(2,1)} %copy-done) | copy-start | bytes 12582916

commit v3 on v2

v3 whole, which is shorter than its diff:
```python
import jax
import jax.numpy as jnp
from jax import lax
from jax.experimental import pallas as pl
from jax.experimental.pallas import tpu as pltpu
from jax.sharding import PartitionSpec as P

MIB = 1 << 20
F32 = jnp.float32
BF16 = jnp.bfloat16

IN_VMEM = pl.BlockSpec(memory_space=pltpu.VMEM)
IN_SMEM = pl.BlockSpec(memory_space=pltpu.SMEM)
IN_HBM = pl.BlockSpec(memory_space=pltpu.HBM)


def params(mib):
    return pltpu.CompilerParams(vmem_limit_bytes=mib * MIB)


def cost(flops, moved):
    return pl.CostEstimate(flops=flops, bytes_accessed=moved, transcendentals=0)


def hbm(x):
    return pltpu.with_memory_space_constraint(x, pltpu.HBM)


def vmem(x):
    return pltpu.with_memory_space_constraint(x, pltpu.VMEM)


def first_rows_dot(a, b):
    return lax.dot_general(a, b, (((0,), (0,)), ((), ())), preferred_element_type=F32)


def leaves_kernel(
    own_ref, sends_ref, charges_hbm, basis_hbm, up_ref, far_hbm, near_hbm,
    charges, basis, offered, sends, sems, send_sem, out_sems,
):
    chunks = sems.shape[1]
    rows = charges.shape[0] // chunks

    def part(k, which):
        at = pl.ds(k * rows, rows)
        source, target = ((charges_hbm, charges), (basis_hbm, basis))[which]
        return pltpu.make_async_copy(source.at[at], target.at[at], sems.at[which, k])

    listing = pltpu.make_async_copy(sends_ref.at[own_ref[0]], sends, send_sem)
    for k in range(chunks):
        part(k, 0).start()
        part(k, 1).start()
    listing.start()
    for k in range(chunks):
        part(k, 0).wait()
        part(k, 1).wait()

        @pl.loop(0, rows // UP_LEAVES)
        def _(i):
            for c in range(UP_LEAVES):
                n = k * rows + UP_LEAVES * i + c
                up_ref[n] = jnp.dot(basis[n], charges[n], preferred_element_type=F32).astype(BF16)

    listing.wait()

    parts = out_sems.shape[1]
    count = offered.shape[1] // parts

    def result(which, k):
        at = pl.ds(k * count, count)
        target = (far_hbm, near_hbm)[which]
        return pltpu.make_async_copy(offered.at[which, at], target.at[at], out_sems.at[which, k])

    odd = lax.rem(own_ref[0], 2)
    for which, listed in enumerate((odd, 1 - odd)):
        for k in range(parts):

            @pl.loop(0, count // 16)
            def _(i):
                for c in range(16):
                    row = k * count + 16 * i + c
                    offered[which, row] = up_ref[sends[listed, row]]

            result(which, k).start()
    for which in range(2):
        for k in range(parts):
            result(which, k).wait()


UP_LEAVES = 32


def leaf_coefficients(own, leaf_sends, charges, basis_in):
    per_dev, points, rhs = charges.shape
    rank = basis_in.shape[1]
    side = leaf_sends.shape[2]
    chunks = 8
    return pl.pallas_call(
        leaves_kernel,
        in_specs=[IN_SMEM, IN_HBM, IN_HBM, IN_HBM],
        out_specs=[IN_VMEM, IN_HBM, IN_HBM],
        out_shape=[
            pltpu.VMEM((per_dev, rank, rhs), BF16),
            pltpu.HBM((side, rank, rhs), BF16),
            pltpu.HBM((side, rank, rhs), BF16),
        ],
        scratch_shapes=[
            pltpu.VMEM((per_dev, points, rhs), BF16),
            pltpu.VMEM((per_dev, rank, points), BF16),
            pltpu.VMEM((2, side, rank, rhs), BF16),
            pltpu.SMEM((2, side), jnp.int32),
            pltpu.SemaphoreType.DMA((2, chunks)),
            pltpu.SemaphoreType.DMA,
            pltpu.SemaphoreType.DMA((2, 2)),
        ],
        compiler_params=params(28),
        cost_estimate=cost(2 * per_dev * rank * points * rhs, 20 * MIB),
        name="leaf_coefficients",
    )(own, hbm(leaf_sends), hbm(charges), hbm(basis_in))


def parents_kernel(
    own_ref, sends_ref, transfer_hbm, leaf_ref, up_ref, offered_hbm,
    transfer, offered, sends, sems, send_sem, offer_sem,
):
    chunks = sems.shape[0]
    parents, _, rank, _ = transfer.shape
    rhs = leaf_ref.shape[2]
    rows = parents // chunks

    def part(k):
        at = pl.ds(k * rows, rows)
        return pltpu.make_async_copy(transfer_hbm.at[at], transfer.at[at], sems.at[k])

    own = own_ref[0]
    first = pl.multiple_of((own // 8) * 8, 8)
    listing = pltpu.make_async_copy(sends_ref.at[pl.ds(first, 8)], sends, send_sem)
    for k in range(chunks):
        part(k).start()
    listing.start()
    for k in range(chunks):
        part(k).wait()

        @pl.loop(0, rows // PARENTS)
        def _(i):
            for c in range(PARENTS):
                p = k * rows + PARENTS * i + c
                below = leaf_ref[pl.ds(8 * p, 8)].reshape(8 * rank, rhs)
                up_ref[p] = first_rows_dot(transfer[p].reshape(8 * rank, rank), below).astype(BF16)

    listing.wait()
    row = lax.rem(own, 8)

    @pl.loop(0, offered.shape[0] // 16)
    def _(i):
        for c in range(16):
            offered[16 * i + c] = up_ref[sends[row, 16 * i + c]]

    offer = pltpu.make_async_copy(offered, offered_hbm, offer_sem)
    offer.start()
    offer.wait()


PARENTS = 8


def parent_coefficients(own, parent_sends, transfer, up_leaf):
    parents, _, rank, _ = transfer.shape
    rhs = up_leaf.shape[2]
    count_dev = parent_sends.shape[0]
    chunks = 4
    return pl.pallas_call(
        parents_kernel,
        in_specs=[IN_SMEM, IN_HBM, IN_HBM, IN_VMEM],
        out_specs=[IN_VMEM, IN_HBM],
        out_shape=[
            pltpu.VMEM((parents, rank, rhs), BF16),
            pltpu.HBM((count_dev, rank, rhs), BF16),
        ],
        scratch_shapes=[
            pltpu.VMEM(transfer.shape, BF16),
            pltpu.VMEM((count_dev, rank, rhs), BF16),
            pltpu.SMEM((8, count_dev), jnp.int32),
            pltpu.SemaphoreType.DMA((chunks,)),
            pltpu.SemaphoreType.DMA,
            pltpu.SemaphoreType.DMA,
        ],
        compiler_params=params(16),
        cost_estimate=cost(16 * parents * rank * rank * rhs, 8 * MIB),
        name="parent_coefficients",
    )(own, hbm(parent_sends), hbm(transfer), vmem(up_leaf))


def joined_kernel(
    offered_hbm, transfer_hbm, basis_hbm, joined_hbm, same_hbm, transfer, basis, joined, sems, out_sems
):
    chunks = out_sems.shape[0]
    rows = transfer.shape[0] // chunks

    def part(k, which):
        if which:
            at = pl.ds(8 * k * rows, 8 * rows)
            return pltpu.make_async_copy(basis_hbm.at[at], basis.at[at], sems.at[1, k])
        at = pl.ds(k * rows, rows)
        return pltpu.make_async_copy(transfer_hbm.at[at], transfer.at[at], sems.at[0, k])

    def result(k):
        at = pl.ds(8 * k * rows, 8 * rows)
        return pltpu.make_async_copy(joined.at[at], joined_hbm.at[at], out_sems.at[k])

    for k in range(chunks):
        part(k, 0).start()
        part(k, 1).start()
    for k in range(chunks):
        part(k, 0).wait()
        part(k, 1).wait()

        @pl.loop(0, rows // JOINED)
        def _(i):
            for c in range(8 * JOINED):
                p = k * rows + JOINED * i + c // 8
                n = 8 * (k * rows + JOINED * i) + c
                pushed = first_rows_dot(transfer[p, c % 8], basis[n]).astype(BF16)
                joined[n] = jnp.concatenate([basis[n], pushed], axis=0).T

        result(k).start()
    for k in range(chunks):
        result(k).wait()


JOINED = 4


def joined_rows(offered, transfer, basis_out):
    parents, _, rank, _ = transfer.shape
    per_dev, _, points = basis_out.shape
    chunks = 4
    return pl.pallas_call(
        joined_kernel,
        in_specs=[IN_HBM, IN_HBM, IN_HBM],
        out_specs=[IN_HBM, IN_HBM],
        out_shape=[
            pltpu.HBM((per_dev, points, 2 * rank), BF16),
            pltpu.HBM(offered.shape, offered.dtype),
        ],
        input_output_aliases={0: 1},
        scratch_shapes=[
            pltpu.VMEM(transfer.shape, BF16),
            pltpu.VMEM(basis_out.shape, BF16),
            pltpu.VMEM((per_dev, points, 2 * rank), BF16),
            pltpu.SemaphoreType.DMA((2, chunks)),
            pltpu.SemaphoreType.DMA((chunks,)),
        ],
        compiler_params=params(28),
        cost_estimate=cost(2 * per_dev * points * rank * rank, 20 * MIB),
        name="joined_rows",
    )(hbm(offered), hbm(transfer), hbm(basis_out))


def list_fields(sources_ref, stacked, pool, first, count):
    width = sources_ref.shape[0]
    tiles = [
        jnp.concatenate([pool[sources_ref[j, first + q]] for j in range(width)], axis=0)
        for q in range(count)
    ]
    return jnp.dot(stacked, jnp.concatenate(tiles, axis=1), preferred_element_type=F32)


def fill(pool, *parts):
    for part, first in parts:

        @pl.loop(0, part.shape[0] // 8)
        def _(i):
            for c in range(8):
                pool[first + 8 * i + c] = part[8 * i + c]

    pool[pool.shape[0] - 1] = jnp.zeros(pool.shape[1:], pool.dtype)


def far_slots(far, is_far, rows_ref, slots_ref, keys_ref):
    width, targets = far.shape
    one = jnp.where(is_far, 1.0, 0.0)
    slot = lax.broadcasted_iota(jnp.int32, (width, targets), 0)
    earlier = lax.broadcasted_iota(jnp.int32, (width, width), 0) > lax.broadcasted_iota(
        jnp.int32, (width, width), 1
    )
    before = jnp.dot(
        jnp.where(earlier, 1.0, 0.0).astype(BF16), one.astype(BF16), preferred_element_type=F32
    ).astype(jnp.int32)
    for place in range(width):
        here = is_far & (before == place)
        slots_ref[place : place + 1] = jnp.min(
            jnp.where(here, slot, width), axis=0, keepdims=True
        )
        rows_ref[place : place + 1] = jnp.max(jnp.where(here, far, 0), axis=0, keepdims=True)
    used = jnp.sum(one, axis=0, keepdims=True)
    key = used * targets + lax.broadcasted_iota(jnp.int32, (1, targets), 1).astype(F32)
    across = jnp.broadcast_to(key, (targets, targets))
    down = across.T
    rank = jnp.sum(jnp.where(across > down, 1.0, 0.0), axis=1, keepdims=True).astype(jnp.int32)
    at = lax.broadcasted_iota(jnp.int32, (targets, targets), 1)
    keys = jnp.sum(jnp.where(rank == at, down, 0.0), axis=0, keepdims=True)
    keys_ref[...] = keys.astype(jnp.int32)


def lists_kernel(
    device_ref, early_ref, sources_ref, counts_ref, stacked_ref, own_hbm, near_ref,
    field_ref, rows_ref, slots_ref, keys_ref, pool, sem,
):
    own_rows, _, rhs = own_hbm.shape
    side = near_ref.shape[0]
    copy = pltpu.make_async_copy(own_hbm, pool.at[pl.ds(0, own_rows)], sem)
    copy.start()
    fill(pool, (near_ref, own_rows))
    sources = sources_ref[...]
    slot = lax.broadcasted_iota(jnp.int32, sources.shape, 0)
    far = sources - (own_rows + lax.rem(device_ref[0], 2) * side)
    is_far = (slot < counts_ref[...]) & (far >= 0) & (far < side)
    far_slots(far, is_far, rows_ref, slots_ref, keys_ref)
    copy.wait()

    @pl.loop(0, own_rows // LISTS)
    def _(i):
        lists = list_fields(early_ref, stacked_ref[...], pool, LISTS * i, LISTS)
        for q in range(LISTS):
            field_ref[LISTS * i + q] = lists[:, q * rhs : (q + 1) * rhs]


LISTS = 16


def leaf_lists(device, early, sources, counts, stacked, own, near):
    per_dev, rank, rhs = own.shape
    rows = own.shape[0] + near.shape[0]
    return pl.pallas_call(
        lists_kernel,
        in_specs=[IN_SMEM, IN_SMEM, IN_VMEM, IN_VMEM, IN_VMEM, IN_HBM, IN_VMEM],
        out_specs=[IN_VMEM] * 4,
        out_shape=[
            pltpu.VMEM((per_dev, rank, rhs), F32),
            jax.ShapeDtypeStruct(sources.shape, jnp.int32),
            jax.ShapeDtypeStruct(sources.shape, jnp.int32),
            jax.ShapeDtypeStruct((1, per_dev), jnp.int32),
        ],
        scratch_shapes=[
            pltpu.VMEM((rows + 1, rank, rhs), BF16),
            pltpu.SemaphoreType.DMA,
        ],
        compiler_params=params(32),
        cost_estimate=cost(2 * per_dev * sources.shape[0] * rank * rank * rhs, 12 * MIB),
        name="leaf_lists",
    )(device, early, sources, counts, stacked, hbm(own), vmem(near))


def far_kernel(
    keys_ref, rows_ref, slots_ref, wide_ref, far_ref, partial_ref, field_hbm, total, field, sem
):
    block = total.shape[0]
    per_dev = field.shape[0]

    def products(t, g):
        blocks = [
            wide_ref[0, slots_ref[4 * g + i, t]] + wide_ref[1, slots_ref[4 * g + i + 1, t]]
            for i in (0, 2)
        ]
        tiles = [far_ref[rows_ref[4 * g + i, t]] for i in range(4)]
        return jnp.dot(
            jnp.concatenate(blocks, axis=1),
            jnp.concatenate(tiles, axis=0),
            preferred_element_type=F32,
        )

    @pl.loop(0, per_dev // block)
    def _(b):
        targets = [lax.rem(keys_ref[0, block * b + q], per_dev) for q in range(block)]
        most = lax.div(keys_ref[0, block * b], per_dev)

        for q, t in enumerate(targets):
            total[q] = partial_ref[t] + products(t, 0)

        @pl.loop(1, lax.div(most + 3, 4))
        def _(g):
            for q, t in enumerate(targets):
                total[q] += products(t, g)

        for q, t in enumerate(targets):
            field[t] = total[q].astype(BF16)
            pltpu.make_async_copy(field.at[t], field_hbm.at[t], sem).start()

    pltpu.make_async_copy(field, field_hbm, sem).wait()


FAR = 32


def far_lists(keys, rows, slots, wide, far, partial):
    per_dev, rank, rhs = partial.shape
    return pl.pallas_call(
        far_kernel,
        in_specs=[IN_SMEM, IN_SMEM, IN_SMEM, IN_VMEM, IN_VMEM, IN_VMEM],
        out_specs=IN_HBM,
        out_shape=pltpu.HBM((per_dev, rank, rhs), BF16),
        scratch_shapes=[
            pltpu.VMEM((FAR, rank, rhs), F32),
            pltpu.VMEM((per_dev, rank, rhs), BF16),
            pltpu.SemaphoreType.DMA,
        ],
        compiler_params=params(24),
        cost_estimate=cost(8 * per_dev * rank * rank * rhs, 20 * MIB),
        name="far_lists",
    )(keys, rows, slots, wide, vmem(far), vmem(partial))


def down_kernel(
    sources_ref, stacked_ref, own_ref, arrived_ref, field_hbm, joined_hbm, potential_hbm,
    pool, down, field, joined, potential, sems, out_sems,
):
    chunks = out_sems.shape[0]
    parents, _, rhs = own_ref.shape
    rows = joined.shape[0] // chunks

    def part(k, which):
        at = pl.ds(k * rows, rows)
        source, target = ((field_hbm, field), (joined_hbm, joined))[which]
        return pltpu.make_async_copy(source.at[at], target.at[at], sems.at[which, k])

    def result(k):
        at = pl.ds(k * rows, rows)
        return pltpu.make_async_copy(potential.at[at], potential_hbm.at[at], out_sems.at[k])

    for k in range(chunks):
        part(k, 0).start()
        part(k, 1).start()
    fill(pool, (own_ref, 0), (arrived_ref, parents))

    @pl.loop(0, parents // DOWN_LISTS)
    def _(i):
        lists = list_fields(sources_ref, stacked_ref[...], pool, DOWN_LISTS * i, DOWN_LISTS)
        for q in range(DOWN_LISTS):
            down[DOWN_LISTS * i + q] = lists[:, q * rhs : (q + 1) * rhs].astype(BF16)

    for k in range(chunks):
        part(k, 0).wait()
        part(k, 1).wait()

        @pl.loop(0, rows // (8 * DOWN_PARENTS))
        def _(i):
            for q in range(DOWN_PARENTS):
                p = k * (rows // 8) + DOWN_PARENTS * i + q
                for c in range(8):
                    n = 8 * p + c
                    both = jnp.concatenate([field[n], down[p]], axis=0)
                    potential[n] = jnp.dot(joined[n], both, preferred_element_type=F32).astype(BF16)

        result(k).start()
    for k in range(chunks):
        result(k).wait()


DOWN_LISTS = 4
DOWN_PARENTS = 4
DOWN_CHUNKS = 8


def downward(sources, stacked, own, arrived, field, joined):
    parents, rank, rhs = own.shape
    per_dev, points, _ = joined.shape
    rows = own.shape[0] + arrived.shape[0]
    chunks = DOWN_CHUNKS
    return pl.pallas_call(
        down_kernel,
        in_specs=[IN_SMEM, IN_VMEM, IN_VMEM, IN_VMEM, IN_HBM, IN_HBM],
        out_specs=IN_HBM,
        out_shape=pltpu.HBM((per_dev, points, rhs), BF16),
        scratch_shapes=[
            pltpu.VMEM((rows + 1, rank, rhs), BF16),
            pltpu.VMEM((parents, rank, rhs), BF16),
            pltpu.VMEM(field.shape, BF16),
            pltpu.VMEM(joined.shape, BF16),
            pltpu.VMEM((per_dev, points, rhs), BF16),
            pltpu.SemaphoreType.DMA((2, chunks)),
            pltpu.SemaphoreType.DMA((chunks,)),
        ],
        compiler_params=params(40),
        cost_estimate=cost(6 * per_dev * points * rank * rhs, 24 * MIB),
        name="downward",
    )(sources, stacked, vmem(own), vmem(arrived), hbm(field), hbm(joined))


def side_by_side(coupling):
    width, rank, inner = coupling.shape
    return jnp.transpose(coupling, (1, 0, 2)).reshape(rank, width * inner)


def both_halves(coupling):
    inner = coupling.shape[2]
    blocks = jnp.pad(coupling, ((0, 1), (0, 0), (0, 0)))
    return jnp.stack(
        [
            jnp.pad(blocks, ((0, 0), (0, 0), (0, inner))),
            jnp.pad(blocks, ((0, 0), (0, 0), (inner, 0))),
        ]
    )


def used_slots(sources, counts, zero_row):
    slots = lax.broadcasted_iota(jnp.int32, sources.shape[::-1], 0)
    return jnp.where(slots < counts[None, :], sources.T, zero_row)


def shards(
    charges,
    basis_in,
    basis_out,
    transfer,
    leaf_coupling,
    parent_coupling,
    leaf_sources,
    leaf_counts,
    leaf_sends,
    parent_sources,
    parent_counts,
    parent_sends,
):
    size = lax.axis_size("leaf")
    own = lax.axis_index("leaf").astype(jnp.int32).reshape(1)
    on_chip = [(i, i ^ 1) for i in range(size)]
    off_chip = [(i, i + 1) for i in range(1, size - 1, 2)]
    off_chip += [(j, i) for i, j in off_chip]
    up_leaf, far, near = leaf_coefficients(own, leaf_sends, charges, basis_in)
    from_far = lax.ppermute(far, "leaf", off_chip)
    from_near = lax.ppermute(near, "leaf", on_chip)
    up_parent, offered = parent_coefficients(own, parent_sends, transfer, up_leaf)
    joined, offered = joined_rows(offered, transfer, basis_out)
    arrived = lax.all_to_all(offered, "leaf", split_axis=0, concat_axis=0, tiled=True)
    own_rows, side = up_leaf.shape[0], far.shape[0]
    odd = own[0] % 2
    far_first = own_rows + odd * side
    near_first = own_rows + (1 - odd) * side
    sources = leaf_sources.T
    used = lax.broadcasted_iota(jnp.int32, sources.shape, 0) < leaf_counts[None, :]
    is_far = used & (sources >= far_first) & (sources < far_first + side)
    is_near = sources >= own_rows
    early = jnp.where(is_near, sources - near_first + own_rows, sources)
    early = jnp.where(used & ~is_far, early, own_rows + side)
    partial, far_rows, slots, keys = leaf_lists(
        own, early, sources, leaf_counts[None, :], side_by_side(leaf_coupling), up_leaf, from_near
    )
    field = far_lists(keys, far_rows, slots, both_halves(leaf_coupling), from_far, partial)
    return downward(
        used_slots(parent_sources, parent_counts, up_parent.shape[0] + offered.shape[0]),
        side_by_side(parent_coupling),
        up_parent,
        arrived,
        field,
        joined,
    )


def solution(mesh):
    return jax.shard_map(
        shards,
        mesh=mesh,
        in_specs=(
            P("leaf", None, None),
            P("leaf", None, None),
            P("leaf", None, None),
            P("leaf", None, None, None),
            P(),
            P(),
            P("leaf", None),
            P("leaf"),
            P(),
            P("leaf", None),
            P("leaf"),
            P(),
        ),
        out_specs=P("leaf", None, None),
        check_vma=False,
    )
```

time: 79.7 us -> 74.3 us (0.932)
  waiting for transfers between devices: 7.57 us -> 3.55 us
  Pallas kernels: 51.6 us -> 54.9 us
  starting transfers between devices: 16.1 us -> 13.7 us
  local copies, waits for them, and re-layouts: 2.97 us -> 1.03 us
    pallas_call x2 -> x4, Pallas kernels: 34.8 us -> 39.3 us  [the longest x1 17.4 us: leaf_lists(): pl.pallas_call(lists_kernel, in_specs=[IN_SMEM, IN_SMEM, IN_VMEM, IN_VMEM...]
    all_to_all x1, waiting for transfers between devices: 7.57 us -> 3.54 us  [shards(): lax.all_to_all(offered, 'leaf', split_axis=0, concat_axis=0, tiled=True)]
    unnamed x16 -> x14, local copies, waits for them, and re-layouts: 2.23 us -> 0.04 us
    ppermute x2, starting transfers between devices: 7.67 us -> 6.09 us  [the longest x1 6.01 us: shards(): from_far = lax.ppermute(far, 'leaf', off_chip)]
    pallas_call x1, Pallas kernels: 9.09 us -> 8.23 us  [downward(): pl.pallas_call(down_kernel, in_specs=[IN_SMEM, IN_VMEM, IN_VMEM, IN_VMEM,...]
    all_to_all x1, starting transfers between devices: 8.43 us -> 7.63 us  [shards(): lax.all_to_all(offered, 'leaf', split_axis=0, concat_axis=0, tiled=True)]
  transfers between devices with their start and end apart: 3 -> 3, of which waited for: 1 -> 1; matrix products, arithmetic and copies ran while one was open for 1% -> 1% of each run, Pallas kernels for 44% -> 53%
where the time goes in v3:
time: 74.3 us; the launch traced here: 73.7 us
  Pallas kernels  54.9 us (74%)
  starting transfers between devices  13.7 us (18%)
  waiting for transfers between devices  3.55 us (5%)
  local copies, waits for them, and re-layouts  1.03 us (1%)
    pallas_call x1, Pallas kernels, leaf_lists(): pl.pallas_call(lists_kernel, in_specs=[IN_SMEM, IN_SMEM, IN_VMEM, IN_VMEM...  17.4 us
    pallas_call x1, Pallas kernels, far_lists(): pl.pallas_call(far_kernel, in_specs=[IN_SMEM, IN_SMEM, IN_SMEM, IN_VMEM,...  9.13 us
    pallas_call x1, Pallas kernels, downward(): pl.pallas_call(down_kernel, in_specs=[IN_SMEM, IN_VMEM, IN_VMEM, IN_VMEM,...  8.23 us
    pallas_call x1, Pallas kernels, joined_rows(): pl.pallas_call(joined_kernel, in_specs=[IN_HBM, IN_HBM, IN_HBM], out_spec...  7.79 us
    all_to_all x1, starting transfers between devices, shards(): lax.all_to_all(offered, 'leaf', split_axis=0, concat_axis=0, tiled=True)  7.63 us
    pallas_call x1, Pallas kernels, leaf_coefficients(): pl.pallas_call(leaves_kernel, in_specs=[IN_SMEM, IN_HBM, IN_HBM, IN_HBM],...  7.3 us
    ppermute x1, starting transfers between devices, shards(): from_far = lax.ppermute(far, 'leaf', off_chip)  6.01 us
    pallas_call x1, Pallas kernels, parent_coefficients(): pl.pallas_call(parents_kernel, in_specs=[IN_SMEM, IN_HBM, IN_HBM, IN_VMEM...  5.01 us
  transfers between devices with their start and end apart: 3, of which 1 were waited for; matrix products, arithmetic and copies ran while one was open for 1% of the time, Pallas kernels for 53%

profile of v3, /device:TPU:2, one launch (start us, length us, event | category | flops | bytes accessed | tf_op | source)
XLA Modules:
  0.0 73.7 jit_solution(11300369441875233975)
XLA Ops:
  0.0 7.3 %leaf_coefficients.1 = (bf16[256,64,128]{2,1,0:T(8,128)(2,1)S(1)}, bf16[128,64,128]{2,1,0:T(8,128)(2,1)}, bf16[128,64,128]{2,1,0:T(8,128)(2,1)}) custom-call(s32[1]{0:T(128)} %bitcast.2.own_ref.device_ref, s32[128,2,128]{2,1,0:T(2,128)} %sends_ref.2, bf16[256,128,128]{2,1,0:T(8,128)(2,1)} %charges_hbm.1, bf16[256,64,128]{2,1,0:T(8,128)(2,1)} %basis_hbm.2), custom_call_target="tpu_custom_call" | custom-call | flops 536870912 | bytes 20971520 | tf_op jit(solution)/shard_map/leaf_coefficients/pallas_call | solution.py:98
  7.3 0.0 copy-start
  7.3 0.1 collective-permute-start
  7.4 6.0 %collective-permute-start.1 = (bf16[128,64,128]{2,1,0:T(8,128)(2,1)}, bf16[128,64,128]{2,1,0:T(8,128)(2,1)}, u32[]{:S(2)}, u32[]{:S(2)}) collective-permute-start(bf16[128,64,128]{2,1,0:T(8,128)(2,1)} %get-tuple-element.24), channel_id=1, source_target_pairs={{1,2},{3,4},{5,6},{7,8},{9,10},{11,12},{13,14},{15,16},{17,18},{19... | collective-permute-start | bytes 6291464 | tf_op jit(solution)/shard_map/ppermute | solution.py:531
  13.4 5.0 %parent_coefficients.1 = (bf16[32,64,128]{2,1,0:T(8,128)(2,1)S(1)}, bf16[128,64,128]{2,1,0:T(8,128)(2,1)}) custom-call(s32[1]{0:T(128)} %bitcast.2.own_ref.device_ref, s32[128,128]{1,0:T(8,128)} %sends_ref.3, bf16[32,8,64,64]{3,2,1,0:T(8,128)(2,1)} %transfer_hbm.3, bf16[256,64,128]{2,1,0:T(8,128)(2,1)S(1)} %get-tuple-element.16.leaf_ref.own_hbm), custom_call_target="tpu_custom_call" | custom-call | flops 268435456 | bytes 8388608 | tf_op jit(solution)/shard_map/parent_coefficients/pallas_call | solution.py:172
  18.5 7.8 %joined_rows.1 = (bf16[256,128,128]{2,1,0:T(8,128)(2,1)}, bf16[128,64,128]{2,1,0:T(8,128)(2,1)}) custom-call(bf16[128,64,128]{2,1,0:T(8,128)(2,1)} %get-tuple-element.18.offered_hbm, bf16[32,8,64,64]{3,2,1,0:T(8,128)(2,1)} %transfer_hbm.3, bf16[256,64,128]{2,1,0:T(8,128)(2,1)} %basis_hbm.3), custom_call_target="tpu_custom_call", output_to_operand_aliasing={{1}: (0, {})} | custom-call | flops 268435456 | bytes 20971520 | tf_op jit(solution)/shard_map/joined_rows/pallas_call | solution.py:238
  26.3 0.0 copy-start.4
  26.3 0.0 copy-start.3
  26.3 0.0 copy-start.5
  26.3 0.0 copy-start.6
  26.3 0.0 copy-start.1
  26.3 0.0 copy-start.2
  26.3 7.6 %all-to-all-start = ((bf16[128,64,128]{2,1,0:T(8,128)(2,1)}), bf16[128,64,128]{2,1,0:T(8,128)(2,1)S(1)}, u32[]{:S(2)}, u32[]{:S(2)}) async-start(bf16[128,64,128]{2,1,0:T(8,128)(2,1)} %get-tuple-element.19), calls=%async_computation | async-start | bytes 4194304 | tf_op jit(solution)/shard_map/all_to_all | solution.py:535
  34.0 0.2 copy.14
  34.2 0.2 reshape.11.stacked_ref
  34.4 0.2 copy.15
  34.6 0.2 reshape.13.stacked_ref
  34.8 0.1 pad.12
  34.8 0.2 pad_bitcast_fusion.1
  35.0 0.1 pad_maximum_fusion.wide_ref
  35.2 17.4 %leaf_lists.1 = (f32[256,64,128]{2,1,0:T(8,128)S(1)}, s32[16,256]{1,0:T(8,128)S(1)}, s32[16,256]{1,0:T(8,128)S(1)}, s32[1,256]{1,0:T(1,128)S(1)}) custom-call(s32[1]{0:T(128)} %bitcast.2.own_ref.device_ref, s32[16,256]{1,0:T(8,128)S(1)} %fusion.early_ref, s32[16,256]{1,0:T(8,128)S(1)} %bitcast.12, s32[1,256]{1,0:T(1,128)S(1)} %bitcast.13, ...), custom_call_target="tpu_custom_call" | custom-call | flops 4294967296 | bytes 12582912 | tf_op jit(solution)/shard_map/leaf_lists/pallas_call | solution.py:335
  52.6 9.1 %far_lists.1.field_hbm = bf16[256,64,128]{2,1,0:T(8,128)(2,1)} custom-call(s32[1,256]{1,0:T(1,128)S(1)} %get-tuple-element.21.keys_ref, s32[16,256]{1,0:T(8,128)S(1)} %get-tuple-element.22.rows_ref, s32[16,256]{1,0:T(8,128)S(1)} %get-tuple-element.23.slots_ref, bf16[2,17,64,128]{3,2,1,0:T(8,128)(2,1)S(1)} %pad_maximum_fusion.wide_ref, ...), custom_call_target="tpu_custom_call" | custom-call | flops 1073741824 | bytes 20971520 | tf_op jit(solution)/shard_map/far_lists/pallas_call | solution.py:398
  61.7 3.5 %all-to-all-done.arrived_ref = bf16[128,64,128]{2,1,0:T(8,128)(2,1)S(1)} async-done(((bf16[128,64,128]{2,1,0:T(8,128)(2,1)}), bf16[128,64,128]{2,1,0:T(8,128)(2,1)S(1)}, u32[]{:S(2)}, u32[]{:S(2)}) %all-to-all-start) | async-done | bytes 2097184 | tf_op jit(solution)/shard_map/all_to_all | solution.py:535
  65.3 8.2 %downward.1 = bf16[256,128,128]{2,1,0:T(8,128)(2,1)} custom-call(s32[16,32]{1,0:T(8,128)S(1)} %bitcast_select_fusion.sources_ref, bf16[64,1024]{1,0:T(8,128)(2,1)S(1)} %reshape.11.stacked_ref, bf16[32,64,128]{2,1,0:T(8,128)(2,1)S(1)} %get-tuple-element.17.own_ref, bf16[128,64,128]{2,1,0:T(8,128)(2,1)S(1)} %all-to-all-done.arrived_ref, ...), custom_call_target="tpu_custom_call" | custom-call | flops 1610612736 | bytes 25165824 | tf_op jit(solution)/shard_map/downward/pallas_call | solution.py:470
  (11 shorter events, 0.0 us)
Async XLA Ops:
  7.3 11.1 %copy-start = (bf16[256,64,128]{2,1,0:T(8,128)(2,1)}, bf16[256,64,128]{2,1,0:T(8,128)(2,1)S(1)}, u32[]{:S(2)}) copy-start(bf16[256,64,128]{2,1,0:T(8,128)(2,1)S(1)} %get-tuple-element.16.leaf_ref.own_hbm) | copy-start | bytes 12582916
  7.3 27.8 %collective-permute-start = (bf16[128,64,128]{2,1,0:T(8,128)(2,1)}, bf16[128,64,128]{2,1,0:T(8,128)(2,1)}, u32[]{:S(2)}, u32[]{:S(2)}) collective-permute-start(bf16[128,64,128]{2,1,0:T(8,128)(2,1)} %get-tuple-element.20), channel_id=1, source_target_pairs={{0,1},{1,0},{2,3},{3,2},{4,5},{5,4},{6,7},{7,6},{8,9},{9,8},{10,11... | collective-permute-start | bytes 6291464 | tf_op jit(solution)/shard_map/ppermute | solution.py:532
  7.4 45.2 %collective-permute-start.1 = (bf16[128,64,128]{2,1,0:T(8,128)(2,1)}, bf16[128,64,128]{2,1,0:T(8,128)(2,1)}, u32[]{:S(2)}, u32[]{:S(2)}) collective-permute-start(bf16[128,64,128]{2,1,0:T(8,128)(2,1)} %get-tuple-element.24), channel_id=1, source_target_pairs={{1,2},{3,4},{5,6},{7,8},{9,10},{11,12},{13,14},{15,16},{17,18},{19... | collective-permute-start | bytes 6291464 | tf_op jit(solution)/shard_map/ppermute | solution.py:531
  26.3 7.7 %copy-start.4 = (bf16[16,64,64]{2,1,0:T(8,128)(2,1)S(1)}, bf16[16,64,64]{2,1,0:T(8,128)(2,1)}, u32[]{:S(2)}) copy-start(bf16[16,64,64]{2,1,0:T(8,128)(2,1)} %param.17) | copy-start | bytes 393220
  26.3 8.1 %copy-start.3 = (bf16[16,64,64]{2,1,0:T(8,128)(2,1)S(1)}, bf16[16,64,64]{2,1,0:T(8,128)(2,1)}, u32[]{:S(2)}) copy-start(bf16[16,64,64]{2,1,0:T(8,128)(2,1)} %param.16) | copy-start | bytes 393220
  26.3 8.8 %copy-start.5 = (s32[32,16]{0,1:T(8,128)S(1)}, s32[32,16]{0,1:T(8,128)}, u32[]{:S(2)}) copy-start(s32[32,16]{0,1:T(8,128)} %param.21) | copy-start | bytes 6148
  26.3 8.8 %copy-start.6 = (s32[32]{0:T(128)S(1)}, s32[32]{0:T(128)}, u32[]{:S(2)}) copy-start(s32[32]{0:T(128)} %param.22) | copy-start | bytes 388
  26.3 8.8 %copy-start.1 = (s32[256,16]{0,1:T(8,128)S(1)}, s32[256,16]{0,1:T(8,128)}, u32[]{:S(2)}) copy-start(s32[256,16]{0,1:T(8,128)} %param.18) | copy-start | bytes 49156
  26.3 8.8 %copy-start.2 = (s32[256]{0:T(256)S(1)}, s32[256]{0:T(256)}, u32[]{:S(2)}) copy-start(s32[256]{0:T(256)} %param.19) | copy-start | bytes 3076
  26.3 38.9 %all-to-all-start = ((bf16[128,64,128]{2,1,0:T(8,128)(2,1)}), bf16[128,64,128]{2,1,0:T(8,128)(2,1)S(1)}, u32[]{:S(2)}, u32[]{:S(2)}) async-start(bf16[128,64,128]{2,1,0:T(8,128)(2,1)} %get-tuple-element.19), calls=%async_computation | async-start | bytes 4194304 | tf_op jit(solution)/shard_map/all_to_all | solution.py:535

commit v4 on v3

--- a/solution.py
+++ b/solution.py
@@ -528,8 +528,8 @@
     off_chip = [(i, i + 1) for i in range(1, size - 1, 2)]
     off_chip += [(j, i) for i, j in off_chip]
     up_leaf, far, near = leaf_coefficients(own, leaf_sends, charges, basis_in)
+    from_near = lax.ppermute(near, "leaf", on_chip)
     from_far = lax.ppermute(far, "leaf", off_chip)
-    from_near = lax.ppermute(near, "leaf", on_chip)
     up_parent, offered = parent_coefficients(own, parent_sends, transfer, up_leaf)
     joined, offered = joined_rows(offered, transfer, basis_out)
     arrived = lax.all_to_all(offered, "leaf", split_axis=0, concat_axis=0, tiled=True)

time: 74.3 us -> 74.3 us (level)
  transfers between devices with their start and end apart: 3 -> 3, of which waited for: 1 -> 1; matrix products, arithmetic and copies ran while one was open for 1% -> 1% of each run, Pallas kernels for 53% -> 54%
where the time goes in v4:
time: 74.3 us; the launch traced here: 73.7 us
  Pallas kernels  55.5 us (75%)
  starting transfers between devices  13.7 us (18%)
  waiting for transfers between devices  2.95 us (4%)
  local copies, waits for them, and re-layouts  1.03 us (1%)
    pallas_call x1, Pallas kernels, leaf_lists(): pl.pallas_call(lists_kernel, in_specs=[IN_SMEM, IN_SMEM, IN_VMEM, IN_VMEM...  17.4 us
    pallas_call x1, Pallas kernels, far_lists(): pl.pallas_call(far_kernel, in_specs=[IN_SMEM, IN_SMEM, IN_SMEM, IN_VMEM,...  9.73 us
    pallas_call x1, Pallas kernels, downward(): pl.pallas_call(down_kernel, in_specs=[IN_SMEM, IN_VMEM, IN_VMEM, IN_VMEM,...  8.23 us
    pallas_call x1, Pallas kernels, joined_rows(): pl.pallas_call(joined_kernel, in_specs=[IN_HBM, IN_HBM, IN_HBM], out_spec...  7.79 us
    all_to_all x1, starting transfers between devices, shards(): lax.all_to_all(offered, 'leaf', split_axis=0, concat_axis=0, tiled=True)  7.63 us
    pallas_call x1, Pallas kernels, leaf_coefficients(): pl.pallas_call(leaves_kernel, in_specs=[IN_SMEM, IN_HBM, IN_HBM, IN_HBM],...  7.3 us
    ppermute x1, starting transfers between devices, shards(): from_far = lax.ppermute(far, 'leaf', off_chip)  6.01 us
    pallas_call x1, Pallas kernels, parent_coefficients(): pl.pallas_call(parents_kernel, in_specs=[IN_SMEM, IN_HBM, IN_HBM, IN_VMEM...  5.01 us
  transfers between devices with their start and end apart: 3, of which 1 were waited for; matrix products, arithmetic and copies ran while one was open for 1% of the time, Pallas kernels for 54%

profile of v4, /device:TPU:2, one launch (start us, length us, event | category | flops | bytes accessed | tf_op | source)
XLA Modules:
  0.0 73.7 jit_solution(11300369441875233975)
XLA Ops:
  0.0 7.3 %leaf_coefficients.1 = (bf16[256,64,128]{2,1,0:T(8,128)(2,1)S(1)}, bf16[128,64,128]{2,1,0:T(8,128)(2,1)}, bf16[128,64,128]{2,1,0:T(8,128)(2,1)}) custom-call(s32[1]{0:T(128)} %bitcast.2.own_ref.device_ref, s32[128,2,128]{2,1,0:T(2,128)} %sends_ref.2, bf16[256,128,128]{2,1,0:T(8,128)(2,1)} %charges_hbm.1, bf16[256,64,128]{2,1,0:T(8,128)(2,1)} %basis_hbm.2), custom_call_target="tpu_custom_call" | custom-call | flops 536870912 | bytes 20971520 | tf_op jit(solution)/shard_map/leaf_coefficients/pallas_call | solution.py:98
  7.3 0.0 copy-start
  7.3 0.1 collective-permute-start
  7.4 6.0 %collective-permute-start.1 = (bf16[128,64,128]{2,1,0:T(8,128)(2,1)}, bf16[128,64,128]{2,1,0:T(8,128)(2,1)}, u32[]{:S(2)}, u32[]{:S(2)}) collective-permute-start(bf16[128,64,128]{2,1,0:T(8,128)(2,1)} %get-tuple-element.24), channel_id=1, source_target_pairs={{1,2},{3,4},{5,6},{7,8},{9,10},{11,12},{13,14},{15,16},{17,18},{19... | collective-permute-start | bytes 6291464 | tf_op jit(solution)/shard_map/ppermute | solution.py:532
  13.4 5.0 %parent_coefficients.1 = (bf16[32,64,128]{2,1,0:T(8,128)(2,1)S(1)}, bf16[128,64,128]{2,1,0:T(8,128)(2,1)}) custom-call(s32[1]{0:T(128)} %bitcast.2.own_ref.device_ref, s32[128,128]{1,0:T(8,128)} %sends_ref.3, bf16[32,8,64,64]{3,2,1,0:T(8,128)(2,1)} %transfer_hbm.3, bf16[256,64,128]{2,1,0:T(8,128)(2,1)S(1)} %get-tuple-element.16.leaf_ref.own_hbm), custom_call_target="tpu_custom_call" | custom-call | flops 268435456 | bytes 8388608 | tf_op jit(solution)/shard_map/parent_coefficients/pallas_call | solution.py:172
  18.5 7.8 %joined_rows.1 = (bf16[256,128,128]{2,1,0:T(8,128)(2,1)}, bf16[128,64,128]{2,1,0:T(8,128)(2,1)}) custom-call(bf16[128,64,128]{2,1,0:T(8,128)(2,1)} %get-tuple-element.18.offered_hbm, bf16[32,8,64,64]{3,2,1,0:T(8,128)(2,1)} %transfer_hbm.3, bf16[256,64,128]{2,1,0:T(8,128)(2,1)} %basis_hbm.3), custom_call_target="tpu_custom_call", output_to_operand_aliasing={{1}: (0, {})} | custom-call | flops 268435456 | bytes 20971520 | tf_op jit(solution)/shard_map/joined_rows/pallas_call | solution.py:238
  26.3 0.0 copy-start.4
  26.3 0.0 copy-start.3
  26.3 0.0 copy-start.5
  26.3 0.0 copy-start.6
  26.3 0.0 copy-start.1
  26.3 0.0 copy-start.2
  26.3 7.6 %all-to-all-start = ((bf16[128,64,128]{2,1,0:T(8,128)(2,1)}), bf16[128,64,128]{2,1,0:T(8,128)(2,1)S(1)}, u32[]{:S(2)}, u32[]{:S(2)}) async-start(bf16[128,64,128]{2,1,0:T(8,128)(2,1)} %get-tuple-element.19), calls=%async_computation | async-start | bytes 4194304 | tf_op jit(solution)/shard_map/all_to_all | solution.py:535
  34.0 0.2 copy.14
  34.2 0.2 reshape.11.stacked_ref
  34.4 0.2 copy.15
  34.6 0.2 reshape.13.stacked_ref
  34.8 0.1 pad.12
  34.8 0.2 pad_bitcast_fusion.1
  35.0 0.1 pad_maximum_fusion.wide_ref
  35.2 17.4 %leaf_lists.1 = (f32[256,64,128]{2,1,0:T(8,128)S(1)}, s32[16,256]{1,0:T(8,128)S(1)}, s32[16,256]{1,0:T(8,128)S(1)}, s32[1,256]{1,0:T(1,128)S(1)}) custom-call(s32[1]{0:T(128)} %bitcast.2.own_ref.device_ref, s32[16,256]{1,0:T(8,128)S(1)} %fusion.early_ref, s32[16,256]{1,0:T(8,128)S(1)} %bitcast.12, s32[1,256]{1,0:T(1,128)S(1)} %bitcast.13, ...), custom_call_target="tpu_custom_call" | custom-call | flops 4294967296 | bytes 12582912 | tf_op jit(solution)/shard_map/leaf_lists/pallas_call | solution.py:335
  52.6 9.7 %far_lists.1.field_hbm = bf16[256,64,128]{2,1,0:T(8,128)(2,1)} custom-call(s32[1,256]{1,0:T(1,128)S(1)} %get-tuple-element.21.keys_ref, s32[16,256]{1,0:T(8,128)S(1)} %get-tuple-element.22.rows_ref, s32[16,256]{1,0:T(8,128)S(1)} %get-tuple-element.23.slots_ref, bf16[2,17,64,128]{3,2,1,0:T(8,128)(2,1)S(1)} %pad_maximum_fusion.wide_ref, ...), custom_call_target="tpu_custom_call" | custom-call | flops 1073741824 | bytes 20971520 | tf_op jit(solution)/shard_map/far_lists/pallas_call | solution.py:398
  62.3 2.9 %all-to-all-done.arrived_ref = bf16[128,64,128]{2,1,0:T(8,128)(2,1)S(1)} async-done(((bf16[128,64,128]{2,1,0:T(8,128)(2,1)}), bf16[128,64,128]{2,1,0:T(8,128)(2,1)S(1)}, u32[]{:S(2)}, u32[]{:S(2)}) %all-to-all-start) | async-done | bytes 2097184 | tf_op jit(solution)/shard_map/all_to_all | solution.py:535
  65.3 8.2 %downward.1 = bf16[256,128,128]{2,1,0:T(8,128)(2,1)} custom-call(s32[16,32]{1,0:T(8,128)S(1)} %bitcast_select_fusion.sources_ref, bf16[64,1024]{1,0:T(8,128)(2,1)S(1)} %reshape.11.stacked_ref, bf16[32,64,128]{2,1,0:T(8,128)(2,1)S(1)} %get-tuple-element.17.own_ref, bf16[128,64,128]{2,1,0:T(8,128)(2,1)S(1)} %all-to-all-done.arrived_ref, ...), custom_call_target="tpu_custom_call" | custom-call | flops 1610612736 | bytes 25165824 | tf_op jit(solution)/shard_map/downward/pallas_call | solution.py:470
  (11 shorter events, 0.0 us)
Async XLA Ops:
  7.3 11.1 %copy-start = (bf16[256,64,128]{2,1,0:T(8,128)(2,1)}, bf16[256,64,128]{2,1,0:T(8,128)(2,1)S(1)}, u32[]{:S(2)}) copy-start(bf16[256,64,128]{2,1,0:T(8,128)(2,1)S(1)} %get-tuple-element.16.leaf_ref.own_hbm) | copy-start | bytes 12582916
  7.3 27.8 %collective-permute-start = (bf16[128,64,128]{2,1,0:T(8,128)(2,1)}, bf16[128,64,128]{2,1,0:T(8,128)(2,1)}, u32[]{:S(2)}, u32[]{:S(2)}) collective-permute-start(bf16[128,64,128]{2,1,0:T(8,128)(2,1)} %get-tuple-element.20), channel_id=1, source_target_pairs={{0,1},{1,0},{2,3},{3,2},{4,5},{5,4},{6,7},{7,6},{8,9},{9,8},{10,11... | collective-permute-start | bytes 6291464 | tf_op jit(solution)/shard_map/ppermute | solution.py:531
  7.4 45.2 %collective-permute-start.1 = (bf16[128,64,128]{2,1,0:T(8,128)(2,1)}, bf16[128,64,128]{2,1,0:T(8,128)(2,1)}, u32[]{:S(2)}, u32[]{:S(2)}) collective-permute-start(bf16[128,64,128]{2,1,0:T(8,128)(2,1)} %get-tuple-element.24), channel_id=1, source_target_pairs={{1,2},{3,4},{5,6},{7,8},{9,10},{11,12},{13,14},{15,16},{17,18},{19... | collective-permute-start | bytes 6291464 | tf_op jit(solution)/shard_map/ppermute | solution.py:532
  26.3 7.7 %copy-start.4 = (bf16[16,64,64]{2,1,0:T(8,128)(2,1)S(1)}, bf16[16,64,64]{2,1,0:T(8,128)(2,1)}, u32[]{:S(2)}) copy-start(bf16[16,64,64]{2,1,0:T(8,128)(2,1)} %param.17) | copy-start | bytes 393220
  26.3 8.1 %copy-start.3 = (bf16[16,64,64]{2,1,0:T(8,128)(2,1)S(1)}, bf16[16,64,64]{2,1,0:T(8,128)(2,1)}, u32[]{:S(2)}) copy-start(bf16[16,64,64]{2,1,0:T(8,128)(2,1)} %param.16) | copy-start | bytes 393220
  26.3 8.8 %copy-start.5 = (s32[32,16]{0,1:T(8,128)S(1)}, s32[32,16]{0,1:T(8,128)}, u32[]{:S(2)}) copy-start(s32[32,16]{0,1:T(8,128)} %param.21) | copy-start | bytes 6148
  26.3 8.8 %copy-start.6 = (s32[32]{0:T(128)S(1)}, s32[32]{0:T(128)}, u32[]{:S(2)}) copy-start(s32[32]{0:T(128)} %param.22) | copy-start | bytes 388
  26.3 8.8 %copy-start.1 = (s32[256,16]{0,1:T(8,128)S(1)}, s32[256,16]{0,1:T(8,128)}, u32[]{:S(2)}) copy-start(s32[256,16]{0,1:T(8,128)} %param.18) | copy-start | bytes 49156
  26.3 8.8 %copy-start.2 = (s32[256]{0:T(256)S(1)}, s32[256]{0:T(256)}, u32[]{:S(2)}) copy-start(s32[256]{0:T(256)} %param.19) | copy-start | bytes 3076
  26.3 38.9 %all-to-all-start = ((bf16[128,64,128]{2,1,0:T(8,128)(2,1)}), bf16[128,64,128]{2,1,0:T(8,128)(2,1)S(1)}, u32[]{:S(2)}, u32[]{:S(2)}) async-start(bf16[128,64,128]{2,1,0:T(8,128)(2,1)} %get-tuple-element.19), calls=%async_computation | async-start | bytes 4194304 | tf_op jit(solution)/shard_map/all_to_all | solution.py:535
